TPU v7x, 32 devices: a whole 2x2x4 slice. The times are simulated.
32 devices in a mesh: tm: 8 (over z, y), chan: 4 (over x, core).
Axes of the slice: x: 2, y: 2, z: 4, core: 2. Of those that a mesh axis runs over, the one named last changes fastest.
Arguments:
- tokens: bfloat16 [8, 2048, 2048], P(None, 'tm', 'chan'), may hold values from -6 to 6
- ln_gain: float32 [2048], replicated, may hold values from 0.5 to 1.5
- ln_bias: float32 [2048], replicated, may hold values from -1.5 to 1.5
- weights: bfloat16 [3, 2048, 2048], P(None, None, 'chan'), may hold values from -0.125 to 0.125
- mix_forget: float32 [2048], P('chan'), may hold values from -0.5 to 0.5
- mix_reset: float32 [2048], P('chan'), may hold values from -1 to 1
- bias_forget: float32 [2048], P('chan'), as said below
- bias_reset: float32 [2048], P('chan'), may hold values from -1 to 1
- state_bank: float32 [8, 2048], P(None, 'chan'), may hold values from -6 to 6
- selector: int32 [8], replicated, may hold values from 0 to 7
- resets: int32 [8, 16], replicated, may hold values from 1 to 2048, as said below
- cotangent: bfloat16 [8, 2048, 2048], P(None, 'tm', 'chan'), may hold values from -6 to 6
Outputs:
- activations: bfloat16 [8, 2048, 2048], P(None, 'tm', 'chan')
- final_states: float32 [8, 2048], P(None, 'chan')
- input_grad: float32 [8, 2048, 2048], P(None, 'tm', 'chan')
- weight_grad: float32 [3, 2048, 2048], P(None, None, 'chan')
- gain_grad: float32 [2048], P('chan')
- norm_bias_grad: float32 [2048], P('chan')
- mix_forget_grad: float32 [2048], P('chan')
- mix_reset_grad: float32 [2048], P('chan')
- bias_forget_grad: float32 [2048], P('chan')
- bias_reset_grad: float32 [2048], P('chan')
Inputs may be any that keep to these rules, and one draw needn't show every extreme that they name: `resets`: each row lists 16 positions. In one row all entries equal 2048 (no reset in that row). Every other row begins sentences at o, o + 128, o + 256, ..., with its own offset o from 1 to 127. `bias_forget`: between 1.5 and ln(2048) + 2.
All inputs are finite; a program needn't handle non-finite values.
Results may differ from a plain program's by a relative error of at most 0.0052.
Values may be sent and summed in bfloat16 or wider, within the bound.
A program may use at most 192 MiB of HBM per device.

v0:
```python
import jax
import jax.numpy as jnp
from jax import lax
from jax.experimental import pallas as pl
from jax.experimental.pallas import tpu as pltpu
from jax.sharding import PartitionSpec as P

EPSILON = 1e-05
CHUNK = 32
BLOCK = 16
LANE = 128
UNIT = 256
LAG = 2
SLICE = 7
VMEM_BYTES = 63 << 20
WIDEN = 512
FIRST = 5
MESH = pl.DeviceIdType.MESH
F32 = jnp.float32
BF16 = jnp.bfloat16


def sigmoid(v):
    return 1.0 / (1.0 + jnp.exp(-v))


def swapped(v, outer, inner):
    return jnp.swapaxes(v.reshape(outer, inner, v.shape[-1]), 0, 1).reshape(outer * inner, v.shape[-1])


def both(*conditions):
    out = conditions[0]
    for c in conditions[1:]:
        out = jnp.logical_and(out, c)
    return out


def ring_of(tm_count):
    return 12 if tm_count <= 8 else 3


def layer_kernel(
    tokens, weights, cotangent, gain, shift, mix_f, mix_r, bias_f, bias_r, bank, selector, resets,
    fin, in_grad, act, low_t, final, totals,
    raw, rx, low, low_t_buf, w_buf, cand, forget, gate, masked, own_tok, cot_raw, cot, mean, inv, keep_mask, grad_buf,
    act_buf, side, terms, out_buf, row_rx, more, sum_rx, mean_s, inv_s, part_s, entry, fore, back, flow, reset_rows,
    x_send, x_recv, s_send, s_recv, d_send, d_recv, own_sem, w_sem, cot_sem, act_sem, tr_sem, low_sem,
    fore_send, fore_recv, back_send, back_recv, ready_sem, out_sem, loc_sem, pair_send, pair_recv, red_send, red_recv,
    bc_send, bc_recv, swap_send, swap_recv, give_send, give_recv, sib_send, sib_recv, acr_send, acr_recv, row_send,
    row_recv, sum_send, sum_recv,
):
    rows, steps, width = tokens.shape
    full = gain.shape[-1]
    tm_count, tm = lax.axis_size("tm"), lax.axis_index("tm")
    chan_count, chan = lax.axis_size("chan"), lax.axis_index("chan")
    sibling = chan + 1 - 2 * lax.rem(chan, 2)
    across = lax.rem(chan + 2, 4)
    chunks = steps // CHUNK
    span = CHUNK * rows
    part = BLOCK * rows
    tiles = width // LANE
    blocks = CHUNK // BLOCK
    units = 3 * full // UNIT
    per_gate = full // UNIT
    pieces = UNIT // 4 // CHUNK

    def remote(src, dst, send, recv, target):
        return pltpu.make_async_remote_copy(src, dst, send, recv, device_id=target, device_id_type=MESH)

    def lanes(j):
        return slice(j * LANE, (j + 1) * LANE)

    def mine(ref, j):
        return ref[0:1, pl.ds(pl.multiple_of(chan * width + j * LANE, LANE), LANE)]

    def hat(at, j):
        return (own_tok[at, lanes(j)].astype(F32) - mean[at, :]) * inv[at, :]

    def normed(at, j):
        return hat(at, j) * mine(gain, j) + mine(shift, j)

    def rows_of(ch):
        return pl.ds(pl.multiple_of(ch * span, span), span)

    def piece(ch):
        return tokens.at[:, pl.ds(pl.multiple_of(ch * CHUNK, CHUNK), CHUNK), :]

    def raw_at(ch, block):
        return raw.at[pl.ds(pl.multiple_of((ch * chan_count + block) * rows, rows), rows)]

    def own_copy(ch):
        return pltpu.make_async_copy(piece(ch), raw_at(ch, chan), own_sem.at[ch])

    def x_copy(ch):
        return remote(piece(ch), raw_at(ch, chan), x_send.at[ch], x_recv.at[ch], (tm, across))

    def s_copy(ch):
        return remote(piece(ch), raw_at(ch, chan), s_send.at[ch], s_recv.at[ch], (tm, sibling))

    def d_copy(ch):
        return remote(raw_at(ch, across), raw_at(ch, across), d_send.at[ch], d_recv.at[ch], (tm, sibling))

    def cot_copy(ch):
        at = pl.ds(pl.multiple_of(ch * CHUNK, CHUNK), CHUNK)
        return pltpu.make_async_copy(cotangent.at[:, at, :], cot_raw.at[lax.rem(ch, 2)], cot_sem.at[lax.rem(ch, 2)])

    def act_copy(ch):
        at = pl.ds(pl.multiple_of(ch * CHUNK, CHUNK), CHUNK)
        return pltpu.make_async_copy(act_buf.at[lax.rem(ch, 2)], act.at[:, at, :], act_sem.at[lax.rem(ch, 2)])

    def tr_copy(ch):
        return pltpu.make_async_copy(low_t_buf, low_t.at[:, rows_of(ch)], tr_sem)

    def low_copy(u):
        at = pl.ds(pl.multiple_of(lax.rem(u, per_gate) * UNIT, UNIT), UNIT)
        return pltpu.make_async_copy(low_t.at[at], low.at[lax.rem(u, 2)], low_sem.at[lax.rem(u, 2)])

    w_copies = [pltpu.make_async_copy(weights.at[k], w_buf.at[k], w_sem.at[k]) for k in range(3)]

    barrier = pltpu.get_barrier_semaphore()
    for d in range(1, 4):
        pl.semaphore_signal(barrier, inc=1, device_id=(tm, lax.rem(chan + d, 4)), device_id_type=MESH)

    def greet(d, carry):
        pl.semaphore_signal(barrier, inc=1, device_id=(lax.rem(tm + d, tm_count), chan), device_id_type=MESH)
        return carry

    lax.fori_loop(1, tm_count, greet, 0)
    own_copy(0).start()
    own_copy(1).start()
    cot_copy(0).start()
    for copy in w_copies:
        copy.start()
    pl.semaphore_wait(barrier, tm_count + 2)
    for ch in range(2):
        x_copy(ch).start()
        s_copy(ch).start()

    count = resets.shape[1]
    for j in range(count):
        reset_rows[j] = jnp.broadcast_to(resets[:, j : j + 1], (rows, LANE))

    def mark(t, carry):
        at = tm * steps + t

        def compare(j, hit):
            return jnp.maximum(hit, jnp.where(reset_rows[j] == at, 1.0, 0.0))

        hit = lax.fori_loop(0, count, compare, jnp.zeros((rows, LANE), F32), unroll=16)
        keep_mask[pl.ds(pl.multiple_of(t * rows, rows), rows), :] = 1.0 - hit
        return carry

    lax.fori_loop(0, steps, mark, 0)
    for r in range(rows):
        entry[r : r + 1, :] = bank[pl.ds(selector[r], 1), :]

    def flip(ch):
        @pl.when(ch >= 1)
        def _():
            tr_copy(ch - 1).wait()

        def one(j, carry):
            cols = pl.ds(pl.multiple_of(j * 256, 256), 256)
            low_t_buf[cols, :] = jnp.transpose(low[lax.rem(ch, 2), :, cols])
            return carry

        lax.fori_loop(0, full // 256, one, 0)
        tr_copy(ch).start()

    def gather_step(ch, carry):
        a_run, b_run = carry

        @pl.when(ch + 2 < chunks)
        def _():
            own_copy(ch + 2).start()
            x_copy(ch + 2).start()
            s_copy(ch + 2).start()

        @pl.when(ch + 1 < chunks)
        def _():
            cot_copy(ch + 1).start()

        base = pl.multiple_of(ch * span, span)
        slot = lax.rem(ch, 2)

        cot_copy(ch).wait()
        for h in range(blocks):
            for j in range(tiles):
                v = cot_raw[slot, :, h * BLOCK : (h + 1) * BLOCK, lanes(j)].astype(F32).reshape(part, LANE)
                cot[pl.ds(pl.multiple_of(base + h * part, part), part), lanes(j)] = swapped(v, rows, BLOCK).astype(BF16)
        pl.when(ch >= 1)(lambda: flip(ch - 1))

        x_copy(ch).wait_recv()
        d_copy(ch).start()
        own_copy(ch).wait()
        s_copy(ch).wait_recv()
        d_copy(ch).wait_recv()

        first = pl.multiple_of(ch * chan_count * rows, rows)

        def each(i, turn):
            r, h = i // blocks, lax.rem(i, blocks)
            t0 = pl.multiple_of(h * BLOCK, BLOCK)
            total = jnp.zeros((BLOCK, LANE), F32)
            for b in range(chan_count):
                for j in range(tiles):
                    total = total + turn(raw[first + b * rows + r, pl.ds(t0, BLOCK), lanes(j)].astype(F32), h, r)
            part_s[h, r] = total

        def sum_rows(i, carry):
            each(i, lambda v, h, r: v)
            return carry

        lax.fori_loop(0, rows * blocks, sum_rows, 0)
        mean_s[...] = jnp.broadcast_to(jnp.sum(part_s[...], axis=-1, keepdims=True) * (1.0 / full), mean_s.shape)

        def square_rows(i, carry):
            r, h = i // blocks, lax.rem(i, blocks)
            m = mean_s[h, r]
            each(i, lambda v, h, r: (v - m) * (v - m))
            return carry

        lax.fori_loop(0, rows * blocks, square_rows, 0)
        var = jnp.sum(part_s[...], axis=-1, keepdims=True) * (1.0 / full)
        inv_s[...] = jnp.broadcast_to(lax.rsqrt(var + EPSILON), inv_s.shape)

        for h in range(blocks):
            mean_h = mean_s[h].reshape(part, LANE)
            inv_h = inv_s[h].reshape(part, LANE)

            def normalize(j, carry, h=h, mean_h=mean_h, inv_h=inv_h):
                cols = pl.ds(pl.multiple_of(j * LANE, LANE), LANE)
                where = pl.ds(first + (j // tiles) * rows, rows)
                inner = pl.ds(pl.multiple_of(lax.rem(j, tiles) * LANE, LANE), LANE)
                v = raw[where, h * BLOCK : (h + 1) * BLOCK, inner].astype(F32).reshape(part, LANE)
                v = (v - mean_h) * inv_h * gain[0:1, cols] + shift[0:1, cols]
                low[slot, h * part : (h + 1) * part, cols] = swapped(v, rows, BLOCK).astype(BF16)
                return carry

            lax.fori_loop(0, full // LANE, normalize, 0)
            at = pl.ds(pl.multiple_of(base + h * part, part), part)
            mean[at, :] = swapped(mean_h, rows, BLOCK)
            inv[at, :] = swapped(inv_h, rows, BLOCK)
            for j in range(tiles):
                v = raw[pl.ds(first + chan * rows, rows), h * BLOCK : (h + 1) * BLOCK, lanes(j)]
                own_tok[at, lanes(j)] = swapped(v.astype(F32).reshape(part, LANE), rows, BLOCK).astype(BF16)

        at = pl.ds(base, span)

        @pl.when(ch == 0)
        def _():
            for copy in w_copies:
                copy.wait()

        cand[at, :] = jnp.dot(low[slot], w_buf[0], preferred_element_type=F32)
        forget[at, :] = jnp.dot(low[slot], w_buf[1], preferred_element_type=F32)
        gate[at, :] = jnp.dot(low[slot], w_buf[2], preferred_element_type=F32)

        def gates(b, carry):
            a_list, b_list = list(carry[0]), list(carry[1])
            at = pl.ds(pl.multiple_of(base + b * part, part), part)
            mask = keep_mask[at, :]
            for j in range(tiles):
                cols = lanes(j)
                nrm = normed(at, j)
                f = sigmoid(forget[at, cols] + mix_f[0:1, cols] * nrm + bias_f[0:1, cols])
                o = sigmoid(gate[at, cols] + mix_r[0:1, cols] * nrm + bias_r[0:1, cols])
                forget[at, cols] = f
                gate[at, cols] = o
                inject = (1.0 - f) * cand[at, cols]
                keep = f * mask
                for t in range(BLOCK):
                    now = slice(t * rows, (t + 1) * rows)
                    a_list[j] = a_list[j] * keep[now]
                    b_list[j] = b_list[j] * keep[now] + inject[now]
            return tuple(a_list), tuple(b_list)

        return lax.fori_loop(0, blocks, gates, (a_run, b_run))

    ones = tuple(jnp.ones((rows, LANE), F32) for _ in range(tiles))
    zeros = tuple(jnp.zeros((rows, LANE), F32) for _ in range(tiles))
    a_run, b_run = lax.fori_loop(0, chunks, gather_step, (ones, zeros))

    for j in range(tiles):
        fore[tm, 0, :, lanes(j)] = a_run[j]
        fore[tm, 1, :, lanes(j)] = b_run[j]

    def fore_copy(source, target):
        return remote(fore.at[source], fore.at[source], fore_send.at[target], fore_recv.at[source], (target, chan))

    def back_copy(source, target):
        return remote(back.at[source], back.at[source], back_send.at[target], back_recv.at[source], (target, chan))

    def sum_copy(source, target):
        return remote(sum_rx.at[source], sum_rx.at[source], sum_send.at[target], sum_recv.at[source], (target, chan))

    def peers(act_on):
        def one(d, carry):
            act_on(lax.rem(tm + d, tm_count))
            return carry

        lax.fori_loop(1, tm_count, one, 0)

    peers(lambda p: fore_copy(tm, p).start())
    flip(chunks - 1)
    peers(lambda p: fore_copy(p, tm).wait_recv())

    def carry_on(d, carry):
        state, here = carry
        here = jnp.where(d == tm, state, here)
        return fore[d, 0] * state + fore[d, 1], here

    last, here = lax.fori_loop(0, tm_count, carry_on, (entry[...], entry[...]))
    final[...] = last
    tr_copy(chunks - 1).wait()
    low_copy(0).start()

    def forward(b, carry):
        states, runs, backs, mr, br = [list(v) for v in carry]
        ch, h = b // blocks, lax.rem(b, blocks)
        slot = lax.rem(ch, 2)

        @pl.when(both(h == 0, ch >= 2))
        def _():
            act_copy(ch - 2).wait()

        at = pl.ds(pl.multiple_of(b * part, part), part)
        t0 = pl.multiple_of(h * BLOCK, BLOCK)
        mask = keep_mask[at, :]
        for j in range(tiles):
            cols = lanes(j)
            f = forget[at, cols]
            inject = (1.0 - f) * cand[at, cols]
            before, after = [], []
            c = states[j]
            for t in range(BLOCK):
                now = slice(t * rows, (t + 1) * rows)
                c = c * mask[now]
                before.append(c)
                c = f[now] * c + inject[now]
                after.append(c)
            states[j] = c
            masked[at, cols] = jnp.concatenate(before, axis=0)
            th = jnp.tanh(jnp.concatenate(after, axis=0))
            o = gate[at, cols]
            x = own_tok[at, cols].astype(F32)
            ct = cot[at, cols].astype(F32)
            rest = 1.0 - o
            out = swapped(o * th + rest * x, BLOCK, rows).astype(BF16)
            act_buf[slot, :, pl.ds(t0, BLOCK), cols] = out.reshape(rows, BLOCK, LANE)
            reset_pre = ct * (th - x) * o * rest
            direct = ct * o * (1.0 - th * th)
            side[at, cols] = (ct * rest).astype(BF16)
            grad_buf[2, at, cols] = reset_pre.astype(BF16)
            gate[at, cols] = direct
            weighted = reset_pre * normed(at, j)
            keep = f * mask
            for t in range(BLOCK):
                now = slice(t * rows, (t + 1) * rows)
                runs[j] = runs[j] * keep[now]
                backs[j] = backs[j] + runs[j] * direct[now]
                mr[j] = mr[j] + weighted[now]
                br[j] = br[j] + reset_pre[now]

        @pl.when(h == blocks - 1)
        def _():
            act_copy(ch).start()

        return tuple(states), tuple(runs), tuple(backs), tuple(mr), tuple(br)

    state = tuple(here[:, lanes(j)] for j in range(tiles))
    _, _, backs, mr, br = lax.fori_loop(0, steps // BLOCK, forward, (state, ones, zeros, zeros, zeros))
    for j in range(tiles):
        back[tm, :, lanes(j)] = backs[j]
    peers(lambda p: back_copy(tm, p).start())

    def sent_on(ch, carry):
        d_copy(ch).wait_send()
        return carry

    lax.fori_loop(0, chunks, sent_on, 0)
    for target in (sibling, across):
        pl.semaphore_signal(ready_sem, inc=1, device_id=(tm, target), device_id_type=MESH)
    for j in range(tiles):
        sum_rx[tm, 1:2, lanes(j)] = jnp.sum(mr[j], axis=0, keepdims=True)
        sum_rx[tm, 3:4, lanes(j)] = jnp.sum(br[j], axis=0, keepdims=True)
    sum_rx[tm, 6:8, :] = jnp.zeros((2, width), F32)
    more[...] = jnp.zeros_like(more)

    n = tm_count // 2
    o, y = tm // 2, lax.rem(tm, 2)
    hops = n // 2
    partner = (o * 2 + 1 - y, chan)
    left = ((o - 1) * 2 + y, chan)
    right = ((o + 1) * 2 + y, chan)
    depth = LAG * (2 * hops + 2)
    ring = ring_of(tm_count)
    space = -(-depth // ring)
    lines = [(y, n // 2 - 1 + y, 1), (2, n // 2 - 1, 0), (3, n // 2, 0)]

    def stage(s, number):
        v = s - LAG * number
        if space == 1:
            return v, both(v >= 0, v < units)
        return v // space, both(v >= 0, lax.rem(v, space) == 0, v // space < units)

    def gate_of(u):
        return lax.rem(u // per_gate + 2, 3)

    def fin_at(u, p):
        return fin.at[gate_of(u) * per_gate + lax.rem(u, per_gate), p]

    def wg_rows(u, p):
        return pl.ds((u * 4 + p) * pieces, pieces)

    def wg_at(u, p):
        return raw.at[wg_rows(u, p)]

    def rx_rows(u, place):
        return pl.ds((lax.rem(u, ring) * SLICE + place) * pieces, pieces)

    def rx_at(u, place):
        return rx.at[rx_rows(u, place)]

    def arrival(l, column, way):
        if l == 0:
            return 1 + way
        other = 6 if l == 1 else jnp.where(column == lines[1][1], 6, 3)
        return jnp.where(column == lines[l][1], 3 + way, other)

    def pair_copy(u):
        return remote(wg_at(u, 1 - y), rx_at(u, 0), pair_send.at[u], pair_recv.at[u], partner)

    def red_copy(l, u, to_right):
        way, column = (0, o + 1) if to_right else (1, o - 1)
        return remote(
            wg_at(u, lines[l][0]), rx_at(u, arrival(l, column, way)), red_send.at[l, u], red_recv.at[l, u, way],
            right if to_right else left,
        )

    def red_wait(l, u, way):
        place = arrival(l, o, way)
        remote(rx_at(u, place), rx_at(u, place), red_send.at[l, u], red_recv.at[l, u, way], partner).wait_recv()
        return rx[rx_rows(u, place)].astype(F32)

    def bc_copy(l, u, to_right, src):
        return remote(
            src, fin_at(u, lines[l][0]), bc_send.at[l, u, 1 if to_right else 0], bc_recv.at[l, u],
            right if to_right else left,
        )

    def swap_copy(l, u):
        return remote(wg_at(u, lines[l][0]), rx_at(u, 5), swap_send.at[l - 1, u], swap_recv.at[l - 1, u], partner)

    def give_copy(u, src):
        return remote(src, fin_at(u, y), give_send.at[u], give_recv.at[u], partner)

    def local_copy(l, u):
        return pltpu.make_async_copy(wg_at(u, lines[l][0]), fin_at(u, lines[l][0]), loc_sem.at[l, u])

    def add_to(l, u, *others):
        at = wg_rows(u, lines[l][0])
        total = raw[at].astype(F32)
        for v in others:
            total = total + v
        raw[at] = total.astype(BF16)

    def red_start(l, u):
        c = lines[l][1]
        pl.when(o < c)(lambda: red_copy(l, u, True).start())
        pl.when(o > c)(lambda: red_copy(l, u, False).start())

    def publish(l, u):
        src = wg_at(u, lines[l][0])
        local_copy(l, u).start()
        pl.when(o > 0)(lambda: bc_copy(l, u, False, src).start())
        pl.when(o < n - 1)(lambda: bc_copy(l, u, True, src).start())
        if l == 0:
            give_copy(u, src).start()

    def block_cols(c):
        return pl.ds(pl.multiple_of(c * width, width), width)

    def sib_rows(ch, q):
        return pl.ds(units * 4 * pieces + (lax.rem(ch, 4) * 2 + q) * rows, rows)

    def sib_copy(ch, q):
        slot = lax.rem(ch, 2)
        cols = sibling if q == 0 else lax.rem(sibling + 2, 4)
        return remote(
            terms.at[slot, cols], raw.at[sib_rows(ch, q)], sib_send.at[ch, q], sib_recv.at[ch, q], (tm, sibling)
        )

    def acr_copy(ch):
        return remote(
            terms.at[lax.rem(ch, 2), across], cot_view(ch), acr_send.at[ch], acr_recv.at[ch], (tm, across)
        )

    def cot_view(ch):
        return cot.at[rows_of(ch)].reshape(rows, CHUNK, width)

    def row_copy(ch, source, d):
        return remote(
            row_rx.at[ch, source], row_rx.at[ch, source], row_send.at[ch, d - 1], row_recv.at[ch, source],
            (tm, lax.rem(chan + d, 4)),
        )

    def out_copy(ch):
        at = pl.ds(pl.multiple_of(ch * CHUNK, CHUNK), CHUNK)
        return pltpu.make_async_copy(out_buf.at[lax.rem(ch, 2)], in_grad.at[:, at, :], out_sem.at[lax.rem(ch, 2)])

    def project(ch):
        at = rows_of(ch)
        slot = lax.rem(ch, 2)

        @pl.when(ch == 0)
        def _():
            pl.semaphore_wait(ready_sem, 2)

        @pl.when(ch >= 2)
        def _():
            acr_copy(ch - 2).wait_send()

        for b in range(chan_count):
            total = jnp.zeros((span, width), F32)
            for k in range(3):
                total = total + lax.dot_general(
                    grad_buf[k, at, :], w_buf[k, b * width : (b + 1) * width, :], (((1,), (1,)), ((), ())),
                    preferred_element_type=F32,
                )
            terms[slot, b] = total.astype(BF16).reshape(rows, CHUNK, width)
        sib_copy(ch, 0).start()
        sib_copy(ch, 1).start()

    def chip_sum(ch):
        slot = lax.rem(ch, 2)
        for q in range(2):
            sib_copy(ch, q).wait_recv()
        there = terms[slot, across].astype(F32) + raw[sib_rows(ch, 1)].astype(F32)
        terms[slot, across] = there.astype(BF16)
        acr_copy(ch).start()
        here = terms[slot, chan].astype(F32) + raw[sib_rows(ch, 0)].astype(F32)
        cand[rows_of(ch), :] = here.reshape(span, width)
        for q in range(2):
            sib_copy(ch, q).wait_send()

    def full_sum(ch):
        acr_copy(ch).wait_recv()
        at = rows_of(ch)
        total = jnp.zeros((8, span), F32)
        pick = lax.broadcasted_iota(jnp.int32, (8, LANE), 0)
        for j in range(tiles):
            cols = lanes(j)
            own = grad_buf[1, at, cols].astype(F32) * mix_f[0:1, cols] + grad_buf[2, at, cols].astype(F32) * mix_r[0:1, cols]
            g = cand[at, cols] + cot[at, cols].astype(F32) + own
            cand[at, cols] = g
            weighted = g * hat(at, j)
            for i, v in enumerate((weighted, g)):
                more[i, :, cols] = more[i, :, cols] + jnp.sum(v.reshape(CHUNK, rows, LANE), axis=0)
            for i, v in enumerate((g * mine(gain, j), weighted * mine(gain, j))):
                lead = jnp.where(pick == i, 1.0, 0.0).astype(BF16)
                high = v.astype(BF16)
                low_part = (v - high.astype(F32)).astype(BF16)
                for p in (high, low_part):
                    total = total + lax.dot_general(lead, p, (((1,), (1,)), ((), ())), preferred_element_type=F32)
        row_rx[ch, chan] = total
        for d in range(1, 4):
            row_copy(ch, chan, d).start()

    def finish(ch):
        for d in range(1, 4):
            row_copy(ch, lax.rem(chan + d, 4), d).wait_recv()

        @pl.when(ch >= 2)
        def _():
            out_copy(ch - 2).wait()

        at = rows_of(ch)
        total = (row_rx[ch, 0] + row_rx[ch, 1] + row_rx[ch, 2] + row_rx[ch, 3]) * (1.0 / full)
        columns = jnp.transpose(total)
        first = jnp.broadcast_to(columns[:, 0:1], (span, LANE))
        second = jnp.broadcast_to(columns[:, 1:2], (span, LANE))
        for j in range(tiles):
            cols = lanes(j)
            g = cand[at, cols] * mine(gain, j)
            v = inv[at, :] * (g - first - hat(at, j) * second) + side[at, cols].astype(F32)
            out_buf[lax.rem(ch, 2), :, :, cols] = swapped(v, CHUNK, rows).reshape(rows, CHUNK, LANE)
        out_copy(ch).start()

    def share_sums():
        for i in range(2):
            sum_rx[tm, 2 * i : 2 * i + 1, :] = jnp.sum(flow[1 + i], axis=0, keepdims=True)
            sum_rx[tm, 4 + i : 5 + i, :] = jnp.sum(more[i], axis=0, keepdims=True)
        peers(lambda p: sum_copy(tm, p).start())

    share = steps // BLOCK // (FIRST - 1)

    def start_backward():
        peers(lambda p: back_copy(p, tm).wait_recv())

        def carry_back(i, v):
            d = tm_count - 1 - i
            return jnp.where(d > tm, fore[d, 0] * v + back[d], v)

        flow[0] = lax.fori_loop(0, tm_count, carry_back, jnp.zeros((rows, width), F32))
        flow[1] = jnp.zeros((rows, width), F32)
        flow[2] = jnp.zeros((rows, width), F32)

    def backward(i, carry):
        b = steps // BLOCK - 1 - i
        at = pl.ds(pl.multiple_of(b * part, part), part)
        mask = keep_mask[at, :]
        for j in range(tiles):
            cols = lanes(j)
            f = forget[at, cols]
            keep = f * mask
            direct = gate[at, cols]
            g = flow[0, :, cols]
            adjoint = [None] * BLOCK
            for t in reversed(range(BLOCK)):
                now = slice(t * rows, (t + 1) * rows)
                adjoint[t] = direct[now] + g
                g = keep[now] * adjoint[t]
            flow[0, :, cols] = g
            cand_grad = jnp.concatenate(adjoint, axis=0) * (1.0 - f)
            forget_pre = cand_grad * (masked[at, cols] - cand[at, cols]) * f
            grad_buf[0, at, cols] = cand_grad.astype(BF16)
            grad_buf[1, at, cols] = forget_pre.astype(BF16)
            for i, v in enumerate((forget_pre * normed(at, j), forget_pre)):
                flow[1 + i, :, cols] = flow[1 + i, :, cols] + jnp.sum(v.reshape(BLOCK, rows, LANE), axis=0)
        return carry

    def slot_step(s, carry):
        u, go = stage(s, 2 * hops + 2)
        pl.when(go)(lambda: give_copy(u, wg_at(u, 0)).wait_recv())

        for l in range(3):
            p, c, first = lines[l]
            late = first + hops + (0 if l == 0 else 1)
            u, go = stage(s, late + jnp.abs(o - c))

            @pl.when(both(o != c, go))
            def _(l=l, c=c, u=u):
                here = fin_at(u, lines[l][0])
                bc_copy(l, u, True, here).wait_recv()
                pl.when(both(o < c, o > 0))(lambda: bc_copy(l, u, False, here).start())
                pl.when(both(o > c, o < n - 1))(lambda: bc_copy(l, u, True, here).start())
                if l == 0:
                    give_copy(u, here).start()

            if l > 0:
                u, go = stage(s, late)

                @pl.when(both(o == c, go))
                def _(l=l, u=u):
                    swap_copy(l, u).wait()
                    add_to(l, u, rx[rx_rows(u, 5)].astype(F32))
                    publish(l, u)

            u, go = stage(s, first + hops)

            @pl.when(both(o == c, go))
            def _(l=l, u=u):
                if n > 2:
                    add_to(l, u, red_wait(l, u, 0), red_wait(l, u, 1))
                else:
                    pl.when(o > 0)(lambda: add_to(l, u, red_wait(l, u, 0)))
                    pl.when(o < n - 1)(lambda: add_to(l, u, red_wait(l, u, 1)))
                if l == 0:
                    publish(l, u)
                else:
                    swap_copy(l, u).start()

            hop = jnp.where(o < c, o, n - 1 - o)
            u, go = stage(s, first + hop)

            @pl.when(both(o < c, o > 0, go))
            def _(l=l, u=u):
                add_to(l, u, red_wait(l, u, 0))
                red_copy(l, u, True).start()

            @pl.when(both(o > c, o < n - 1, go))
            def _(l=l, u=u):
                add_to(l, u, red_wait(l, u, 1))
                red_copy(l, u, False).start()

        u, go = stage(s, 1)

        @pl.when(go)
        def _():
            pair_copy(u).wait_recv()
            add_to(0, u, rx[rx_rows(u, 0)].astype(F32))
            pl.when(jnp.logical_or(o == 0, o == n - 1))(lambda: red_start(0, u))

        u0, go0 = stage(s, 0)

        @pl.when(go0)
        def _():
            pl.when(u0 + 1 < units)(lambda: low_copy(u0 + 1).start())
            low_copy(u0).wait()
            g = jnp.dot(low[lax.rem(u0, 2)], grad_buf[gate_of(u0)], preferred_element_type=F32).astype(BF16)
            raw[pl.ds(u0 * 4 * pieces, 4 * pieces)] = g.reshape(4 * pieces, CHUNK, width)
            pair_copy(u0).start()

            @pl.when(jnp.logical_or(o == 0, o == n - 1))
            def _():
                red_start(1, u0)
                red_start(2, u0)

        pl.when(s == 1)(start_backward)

        @pl.when(both(s >= 1, s < FIRST))
        def _():
            lax.fori_loop((s - 1) * share, s * share, backward, 0)

        for job, offset in ((finish, 5), (full_sum, 3), (chip_sum, 1), (project, 0)):
            at = s - FIRST - offset
            pl.when(both(at >= 0, lax.rem(at, 2) == 0, at // 2 < chunks))(lambda job=job, at=at: job(at // 2))
        pl.when(s == FIRST + 2 * chunks + 2)(share_sums)
        return carry

    slots = max((units - 1) * space + depth + 1, FIRST + 2 * chunks + 4)
    lax.fori_loop(0, slots, slot_step, 0)

    def close_unit(u, carry):
        give_copy(u, wg_at(u, 0)).wait_send()
        pair_copy(u).wait_send()
        for l in range(3):
            c = lines[l][1]
            src = wg_at(u, 0)
            pl.when(o != c)(lambda l=l: red_copy(l, u, True).wait_send())
            pl.when(o == c)(lambda l=l: local_copy(l, u).wait())
            pl.when(both(o <= c, o > 0))(lambda l=l: bc_copy(l, u, False, src).wait_send())
            pl.when(both(o >= c, o < n - 1))(lambda l=l: bc_copy(l, u, True, src).wait_send())
        return carry

    lax.fori_loop(0, units, close_unit, 0)

    def close_chunk(ch, carry):
        x_copy(ch).wait_send()
        s_copy(ch).wait_send()
        for d in range(1, 4):
            row_copy(ch, chan, d).wait_send()
        return carry

    lax.fori_loop(0, chunks, close_chunk, 0)
    for ch in (chunks - 2, chunks - 1):
        out_copy(ch).wait()
        act_copy(ch).wait()
        acr_copy(ch).wait_send()
    peers(lambda p: fore_copy(tm, p).wait_send())
    peers(lambda p: back_copy(tm, p).wait_send())
    peers(lambda p: sum_copy(p, tm).wait_recv())
    peers(lambda p: sum_copy(tm, p).wait_send())
    totals[...] = lax.fori_loop(0, tm_count, lambda d, v: v + sum_rx[d], jnp.zeros(totals.shape, F32))


def layer(tokens, weights, cotangent, gain, shift, mix_f, mix_r, bias_f, bias_r, bank, selector, resets):
    rows, steps, width = tokens.shape
    full = gain.shape[-1]
    tm_count, chan_count = lax.axis_size("tm"), lax.axis_size("chan")
    chunks = steps // CHUNK
    span = CHUNK * rows
    count = steps * rows
    units = 3 * full // UNIT
    pieces = UNIT // 4 // CHUNK
    hbm = pl.BlockSpec(memory_space=pl.ANY)
    vmem = pl.BlockSpec(memory_space=pltpu.VMEM)
    smem = pl.BlockSpec(memory_space=pltpu.SMEM)
    dma = pltpu.SemaphoreType.DMA
    stat = pltpu.VMEM((CHUNK // BLOCK, rows, BLOCK, LANE), F32)
    wide = pltpu.VMEM((count, width), F32)
    narrow = pltpu.VMEM((count, LANE), F32)
    short = pltpu.VMEM((count, width), BF16)
    return pl.pallas_call(
        layer_kernel,
        out_shape=(
            jax.ShapeDtypeStruct((units, 4, pieces, CHUNK, width), BF16),
            jax.ShapeDtypeStruct(tokens.shape, F32),
            jax.ShapeDtypeStruct(tokens.shape, BF16),
            jax.ShapeDtypeStruct((full, count), BF16),
            jax.ShapeDtypeStruct((rows, width), F32),
            jax.ShapeDtypeStruct((8, width), F32),
        ),
        in_specs=[hbm, hbm, hbm] + [vmem] * 7 + [smem, vmem],
        out_specs=(hbm, hbm, hbm, hbm, vmem, vmem),
        scratch_shapes=[
            pltpu.VMEM((chunks * chan_count * rows, CHUNK, width), BF16),
            pltpu.VMEM((ring_of(tm_count) * SLICE * pieces, CHUNK, width), BF16),
            pltpu.VMEM((2, span, full), BF16),
            pltpu.VMEM((full, span), BF16),
            pltpu.VMEM((3, full, width), BF16),
            wide, wide, wide, wide,
            short,
            pltpu.VMEM((2, rows, CHUNK, width), BF16),
            short,
            narrow, narrow, narrow,
            pltpu.VMEM((3, count, width), BF16),
            pltpu.VMEM((2, rows, CHUNK, width), BF16),
            short,
            pltpu.VMEM((2, chan_count, rows, CHUNK, width), BF16),
            pltpu.VMEM((2, rows, CHUNK, width), F32),
            pltpu.VMEM((chunks, 4, 8, span), F32),
            pltpu.VMEM((2, rows, width), F32),
            pltpu.VMEM((tm_count, 8, width), F32),
            stat, stat, stat,
            pltpu.VMEM((rows, width), F32),
            pltpu.VMEM((tm_count, 2, rows, width), F32),
            pltpu.VMEM((tm_count, rows, width), F32),
            pltpu.VMEM((3, rows, width), F32),
            pltpu.VMEM((resets.shape[1], rows, LANE), jnp.int32),
            dma((chunks,)), dma((chunks,)), dma((chunks,)), dma((chunks,)), dma((chunks,)), dma((chunks,)), dma((chunks,)),
            dma((3,)), dma((2,)), dma((2,)), dma(()), dma((2,)),
            dma((tm_count,)), dma((tm_count,)), dma((tm_count,)), dma((tm_count,)),
            pltpu.SemaphoreType.REGULAR,
            dma((2,)), dma((3, units)), dma((units,)), dma((units,)),
            dma((3, units)), dma((3, units, 2)), dma((3, units, 2)), dma((3, units)), dma((2, units)), dma((2, units)),
            dma((units,)), dma((units,)), dma((chunks, 2)), dma((chunks, 2)), dma((chunks,)), dma((chunks,)),
            dma((chunks, 3)), dma((chunks, 4)), dma((tm_count,)), dma((tm_count,)),
        ],
        compiler_params=pltpu.CompilerParams(collective_id=0, has_side_effects=True, vmem_limit_bytes=VMEM_BYTES),
        name="whole",
    )(tokens, weights, cotangent, gain, shift, mix_f, mix_r, bias_f, bias_r, bank, selector, resets)


def widen_kernel(narrow, wide):
    wide[...] = narrow[...].astype(F32)


def widen(fin, shape):
    flat = fin.reshape(-1, shape[-1])
    block = pl.BlockSpec((WIDEN, shape[-1]), lambda i: (i, 0))
    out = pl.pallas_call(
        widen_kernel,
        out_shape=jax.ShapeDtypeStruct(flat.shape, F32),
        grid=(flat.shape[0] // WIDEN,),
        in_specs=[block],
        out_specs=block,
        name="tail",
    )(flat)
    return out.reshape(shape)


def body(
    tokens, ln_gain, ln_bias, weights, mix_forget, mix_reset, bias_forget, bias_reset, state_bank, selector, resets, cotangent
):
    fin, in_grad, act, _, final, totals = layer(
        tokens, weights, cotangent, ln_gain[None], ln_bias[None], mix_forget[None], mix_reset[None], bias_forget[None],
        bias_reset[None], state_bank, selector, resets,
    )
    weight_grad = widen(fin, weights.shape)
    return act, final, in_grad, weight_grad, totals[4], totals[5], totals[0], totals[1], totals[2], totals[3]


def solution(mesh):
    placed = (
        P(None, "tm", "chan"), P(), P(), P(None, None, "chan"), P("chan"), P("chan"), P("chan"), P("chan"),
        P(None, "chan"), P(), P(), P(None, "tm", "chan"),
    )
    return jax.shard_map(
        body,
        mesh=mesh,
        in_specs=placed,
        out_specs=(
            P(None, "tm", "chan"), P(None, "chan"), P(None, "tm", "chan"), P(None, None, "chan"),
            P("chan"), P("chan"), P("chan"), P("chan"), P("chan"), P("chan"),
        ),
        check_vma=False,
    )
```

profile of v0, /device:TPU:0, one launch (start us, length us, event | category | flops | bytes accessed | tf_op | source)
XLA Modules:
  0.0 244.6 jit_solution(4186188035161530147)
XLA Ops:
  0.6 227.0 %whole.1 = (bf16[24,4,2,32,512]{4,3,2,1,0:T(8,128)(2,1)}, f32[8,256,512]{2,1,0:T(8,128)}, bf16[8,256,512]{2,1,0:T(8,128)(2,1)}, bf16[2048,2048]{1,0:T(8,128)(2,1)}, f32[8,512]{1,0:T(8,128)}, /*index=5*/f32[8,512]{1,0:T(8,128)}) custom-call(bf16[8,256,512]{2,1,0:T(8,128)(2,1)} %tokens.1, bf16[3,2048,512]{2,1,0:T(8,128)(2,1)} %weights.1, ...), custom_call_target="tpu_custom_call" | custom-call | tf_op jit(solution)/shard_map/whole/pallas_call | solution.py:775
  227.6 1.5 fusion
  229.2 0.0 copy-start.1
  229.2 0.0 copy-start.2
  229.2 10.5 %tail.1 = f32[6144,512]{1,0:T(8,128)} custom-call(bf16[6144,512]{1,0:T(8,128)(2,1)} %bitcast.15), custom_call_target="tpu_custom_call" | custom-call | tf_op jit(solution)/shard_map/tail/pallas_call | solution.py:833
  239.7 0.0 copy-start
  239.7 0.0 copy-done.1
  239.7 1.3 copy.25
  241.0 0.0 copy-done.2
  241.0 0.6 copy.26
  241.6 1.0 copy-done
  242.6 2.0 copy.27
Async XLA Ops:
  229.2 10.5 %copy-start.1 = (bf16[8,256,512]{2,1,0:T(8,128)(2,1)S(1)}, bf16[8,256,512]{2,1,0:T(8,128)(2,1)}, u32[]{:S(2)}) copy-start(bf16[8,256,512]{2,1,0:T(8,128)(2,1)} %get-tuple-element.36) | copy-start | bytes 6291460
  229.2 11.8 %copy-start.2 = (f32[8,512]{1,0:T(8,128)S(1)}, f32[8,512]{1,0:T(8,128)}, u32[]{:S(2)}) copy-start(f32[8,512]{1,0:T(8,128)} %get-tuple-element.37) | copy-start | bytes 49156
  239.7 3.0 %copy-start = (f32[8,256,512]{2,1,0:T(8,128)S(1)}, f32[8,256,512]{2,1,0:T(8,128)}, u32[]{:S(2)}) copy-start(f32[8,256,512]{2,1,0:T(8,128)} %get-tuple-element.38) | copy-start | bytes 12582916
where the time goes:
time: 245 us
  Pallas kernels  237 us (97%)
  local copies, waits for them, and re-layouts  6.51 us (3%)
    pallas_call x1, Pallas kernels, layer(): pl.pallas_call(layer_kernel, out_shape=(jax.ShapeDtypeStruct((units, 4, p...  227 us
    pallas_call x1, Pallas kernels, widen(): pl.pallas_call(widen_kernel, out_shape=jax.ShapeDtypeStruct(flat.shape, F...  10.5 us
    unnamed x9, local copies, waits for them, and re-layouts  4.97 us

commit v1 on v0

--- a/solution.py
+++ b/solution.py
@@ -13,8 +13,9 @@
 LAG = 2
 SLICE = 7
 VMEM_BYTES = 63 << 20
-WIDEN = 512
-FIRST = 5
+TAIL = 12
+LATER = 4
+FIRST = 8
 MESH = pl.DeviceIdType.MESH
 F32 = jnp.float32
 BF16 = jnp.bfloat16
@@ -315,17 +316,9 @@
     tr_copy(chunks - 1).wait()
     low_copy(0).start()
 
-    def forward(b, carry):
-        states, runs, backs, mr, br = [list(v) for v in carry]
-        ch, h = b // blocks, lax.rem(b, blocks)
-        slot = lax.rem(ch, 2)
-
-        @pl.when(both(h == 0, ch >= 2))
-        def _():
-            act_copy(ch - 2).wait()
-
+    def forward(b, states):
+        states = list(states)
         at = pl.ds(pl.multiple_of(b * part, part), part)
-        t0 = pl.multiple_of(h * BLOCK, BLOCK)
         mask = keep_mask[at, :]
         for j in range(tiles):
             cols = lanes(j)
@@ -343,6 +336,33 @@
             masked[at, cols] = jnp.concatenate(before, axis=0)
             th = jnp.tanh(jnp.concatenate(after, axis=0))
             o = gate[at, cols]
+            gate_grad = cot[at, cols].astype(F32) * (th - own_tok[at, cols].astype(F32))
+            grad_buf[2, at, cols] = (gate_grad * o * (1.0 - o)).astype(BF16)
+        return tuple(states)
+
+    lax.fori_loop(0, steps // BLOCK, forward, tuple(here[:, lanes(j)] for j in range(tiles)))
+
+    def start_later():
+        flow[0] = jnp.ones((rows, width), F32)
+        for i in range(1, 4):
+            flow[i] = jnp.zeros((rows, width), F32)
+
+    def later(b, carry):
+        ch, h = b // blocks, lax.rem(b, blocks)
+        slot = lax.rem(ch, 2)
+
+        @pl.when(both(h == 0, ch >= 2))
+        def _():
+            act_copy(ch - 2).wait()
+
+        at = pl.ds(pl.multiple_of(b * part, part), part)
+        t0 = pl.multiple_of(h * BLOCK, BLOCK)
+        mask = keep_mask[at, :]
+        for j in range(tiles):
+            cols = lanes(j)
+            f = forget[at, cols]
+            th = jnp.tanh(f * masked[at, cols] + (1.0 - f) * cand[at, cols])
+            o = gate[at, cols]
             x = own_tok[at, cols].astype(F32)
             ct = cot[at, cols].astype(F32)
             rest = 1.0 - o
@@ -351,41 +371,38 @@
             reset_pre = ct * (th - x) * o * rest
             direct = ct * o * (1.0 - th * th)
             side[at, cols] = (ct * rest).astype(BF16)
-            grad_buf[2, at, cols] = reset_pre.astype(BF16)
             gate[at, cols] = direct
-            weighted = reset_pre * normed(at, j)
             keep = f * mask
+            run, total = flow[0, :, cols], flow[1, :, cols]
             for t in range(BLOCK):
                 now = slice(t * rows, (t + 1) * rows)
-                runs[j] = runs[j] * keep[now]
-                backs[j] = backs[j] + runs[j] * direct[now]
-                mr[j] = mr[j] + weighted[now]
-                br[j] = br[j] + reset_pre[now]
+                run = run * keep[now]
+                total = total + run * direct[now]
+            flow[0, :, cols], flow[1, :, cols] = run, total
+            for i, v in enumerate((reset_pre * normed(at, j), reset_pre)):
+                flow[2 + i, :, cols] = flow[2 + i, :, cols] + jnp.sum(v.reshape(BLOCK, rows, LANE), axis=0)
 
         @pl.when(h == blocks - 1)
         def _():
             act_copy(ch).start()
 
-        return tuple(states), tuple(runs), tuple(backs), tuple(mr), tuple(br)
-
-    state = tuple(here[:, lanes(j)] for j in range(tiles))
-    _, _, backs, mr, br = lax.fori_loop(0, steps // BLOCK, forward, (state, ones, zeros, zeros, zeros))
-    for j in range(tiles):
-        back[tm, :, lanes(j)] = backs[j]
-    peers(lambda p: back_copy(tm, p).start())
+        return carry
+
+    def end_later():
+        back[tm] = flow[1]
+        peers(lambda p: back_copy(tm, p).start())
+        for target in (sibling, across):
+            pl.semaphore_signal(ready_sem, inc=1, device_id=(tm, target), device_id_type=MESH)
+        for i in range(2):
+            sum_rx[tm, 2 * i + 1 : 2 * i + 2, :] = jnp.sum(flow[2 + i], axis=0, keepdims=True)
+        sum_rx[tm, 6:8, :] = jnp.zeros((2, width), F32)
+        more[...] = jnp.zeros_like(more)
 
     def sent_on(ch, carry):
         d_copy(ch).wait_send()
         return carry
 
     lax.fori_loop(0, chunks, sent_on, 0)
-    for target in (sibling, across):
-        pl.semaphore_signal(ready_sem, inc=1, device_id=(tm, target), device_id_type=MESH)
-    for j in range(tiles):
-        sum_rx[tm, 1:2, lanes(j)] = jnp.sum(mr[j], axis=0, keepdims=True)
-        sum_rx[tm, 3:4, lanes(j)] = jnp.sum(br[j], axis=0, keepdims=True)
-    sum_rx[tm, 6:8, :] = jnp.zeros((2, width), F32)
-    more[...] = jnp.zeros_like(more)
 
     n = tm_count // 2
     o, y = tm // 2, lax.rem(tm, 2)
@@ -592,8 +609,6 @@
             sum_rx[tm, 2 * i : 2 * i + 1, :] = jnp.sum(flow[1 + i], axis=0, keepdims=True)
             sum_rx[tm, 4 + i : 5 + i, :] = jnp.sum(more[i], axis=0, keepdims=True)
         peers(lambda p: sum_copy(tm, p).start())
-
-    share = steps // BLOCK // (FIRST - 1)
 
     def start_backward():
         peers(lambda p: back_copy(p, tm).wait_recv())
@@ -707,11 +722,23 @@
                 red_start(1, u0)
                 red_start(2, u0)
 
-        pl.when(s == 1)(start_backward)
-
-        @pl.when(both(s >= 1, s < FIRST))
-        def _():
-            lax.fori_loop((s - 1) * share, s * share, backward, 0)
+        count = steps // BLOCK
+        pl.when(s == 0)(start_later)
+        share = -(-count // LATER)
+        at = s * share
+
+        @pl.when(s < LATER)
+        def _():
+            lax.fori_loop(at, jnp.minimum(at + share, count), later, 0)
+
+        pl.when(s == LATER - 1)(end_later)
+        pl.when(s == LATER + 1)(start_backward)
+        share = -(-count // (FIRST - LATER - 1))
+        at2 = (s - LATER - 1) * share
+
+        @pl.when(both(s > LATER, s < FIRST))
+        def _():
+            lax.fori_loop(at2, jnp.minimum(at2 + share, count), backward, 0)
 
         for job, offset in ((finish, 5), (full_sum, 3), (chip_sum, 1), (project, 0)):
             at = s - FIRST - offset
@@ -807,7 +834,7 @@
             pltpu.VMEM((rows, width), F32),
             pltpu.VMEM((tm_count, 2, rows, width), F32),
             pltpu.VMEM((tm_count, rows, width), F32),
-            pltpu.VMEM((3, rows, width), F32),
+            pltpu.VMEM((4, rows, width), F32),
             pltpu.VMEM((resets.shape[1], rows, LANE), jnp.int32),
             dma((chunks,)), dma((chunks,)), dma((chunks,)), dma((chunks,)), dma((chunks,)), dma((chunks,)), dma((chunks,)),
             dma((3,)), dma((2,)), dma((2,)), dma(()), dma((2,)),
@@ -823,22 +850,76 @@
     )(tokens, weights, cotangent, gain, shift, mix_f, mix_r, bias_f, bias_r, bank, selector, resets)
 
 
-def widen_kernel(narrow, wide):
-    wide[...] = narrow[...].astype(F32)
-
-
-def widen(fin, shape):
-    flat = fin.reshape(-1, shape[-1])
-    block = pl.BlockSpec((WIDEN, shape[-1]), lambda i: (i, 0))
-    out = pl.pallas_call(
-        widen_kernel,
-        out_shape=jax.ShapeDtypeStruct(flat.shape, F32),
-        grid=(flat.shape[0] // WIDEN,),
-        in_specs=[block],
-        out_specs=block,
+def tail_kernel(
+    fin, in_grad, act, final, totals, wide_out, in_out, act_out, final_out, s0, s1, s2, s3, s4, s5,
+    fin_buf, wide_buf, in_buf, act_buf, fin_sem, wide_sem, in_sem, act_sem,
+):
+    parts = fin_sem.shape[0]
+    size = fin.shape[0] // parts
+    rows = in_sem.shape[1]
+
+    def move(src, dst, sem, i, n):
+        at = pl.ds(i * n, n)
+        return pltpu.make_async_copy(src.at[at], dst.at[at], sem)
+
+    loads = [move(fin, fin_buf, fin_sem.at[i], i, size) for i in range(parts)]
+    stores = [move(wide_buf, wide_out, wide_sem.at[i], i, size) for i in range(parts)]
+    pairs = []
+    for src, buf, dst, sem in ((in_grad, in_buf, in_out, in_sem), (act, act_buf, act_out, act_sem)):
+        for r in range(rows):
+            pairs.append((move(src, buf, sem.at[0, r], r, 1), move(buf, dst, sem.at[1, r], r, 1)))
+    for copy in loads:
+        copy.start()
+    for copy, _ in pairs:
+        copy.start()
+    final_out[...] = final[...]
+    for i, ref in enumerate((s0, s1, s2, s3, s4, s5)):
+        ref[...] = totals[i : i + 1, :]
+    for i in range(parts):
+        loads[i].wait()
+
+        def cast(j, carry, i=i):
+            at = pl.ds(pl.multiple_of(i * size + j * 64, 64), 64)
+            wide_buf[at] = fin_buf[at].astype(F32)
+            return carry
+
+        lax.fori_loop(0, size // 64, cast, 0)
+        stores[i].start()
+    for copy, onward in pairs:
+        copy.wait()
+        onward.start()
+    for copy in stores:
+        copy.wait()
+    for _, onward in pairs:
+        onward.wait()
+
+
+def tail(fin, in_grad, act, final, totals):
+    width = fin.shape[-1]
+    flat = fin.reshape(-1, width)
+    rows = in_grad.shape[0]
+    hbm = pl.BlockSpec(memory_space=pl.ANY)
+    vmem = pl.BlockSpec(memory_space=pltpu.VMEM)
+    dma = pltpu.SemaphoreType.DMA
+    line = jax.ShapeDtypeStruct((1, width), F32)
+    return pl.pallas_call(
+        tail_kernel,
+        out_shape=(
+            jax.ShapeDtypeStruct(flat.shape, F32),
+            jax.ShapeDtypeStruct(in_grad.shape, F32),
+            jax.ShapeDtypeStruct(act.shape, BF16),
+            jax.ShapeDtypeStruct(final.shape, F32),
+        ) + (line,) * 6,
+        in_specs=[hbm] * 3 + [vmem] * 2,
+        out_specs=(hbm,) * 3 + (vmem,) * 7,
+        scratch_shapes=[
+            pltpu.VMEM(flat.shape, BF16), pltpu.VMEM(flat.shape, F32),
+            pltpu.VMEM(in_grad.shape, F32), pltpu.VMEM(act.shape, BF16),
+            dma((TAIL,)), dma((TAIL,)), dma((2, rows)), dma((2, rows)),
+        ],
+        compiler_params=pltpu.CompilerParams(vmem_limit_bytes=40 << 20),
         name="tail",
-    )(flat)
-    return out.reshape(shape)
+    )(flat, in_grad, act, final, totals)
 
 
 def body(
@@ -848,8 +929,9 @@
         tokens, weights, cotangent, ln_gain[None], ln_bias[None], mix_forget[None], mix_reset[None], bias_forget[None],
         bias_reset[None], state_bank, selector, resets,
     )
-    weight_grad = widen(fin, weights.shape)
-    return act, final, in_grad, weight_grad, totals[4], totals[5], totals[0], totals[1], totals[2], totals[3]
+    wide, in_grad, act, final, *sums = tail(fin, in_grad, act, final, totals)
+    sums = [v[0] for v in sums]
+    return act, final, in_grad, wide.reshape(weights.shape), sums[4], sums[5], sums[0], sums[1], sums[2], sums[3]
 
 
 def solution(mesh):

time: 245 us -> 241 us (0.984)
  Pallas kernels: 237 us -> 232 us
    pallas_call x1, Pallas kernels: 227 us -> 224 us  [layer(): pl.pallas_call(layer_kernel, out_shape=(jax.ShapeDtypeStruct((units, 4, p...]
    unnamed x9 -> x10, local copies, waits for them, and re-layouts: 4.97 us -> 7.99 us
where the time goes in v1:
time: 241 us
  Pallas kernels  232 us (96%)
  local copies, waits for them, and re-layouts  7.99 us (3%)
    pallas_call x1, Pallas kernels, layer(): pl.pallas_call(layer_kernel, out_shape=(jax.ShapeDtypeStruct((units, 4, p...  224 us
    pallas_call x1, Pallas kernels, tail(): pl.pallas_call(tail_kernel, out_shape=(jax.ShapeDtypeStruct(flat.shape, F...  8.49 us
    unnamed x10, local copies, waits for them, and re-layouts  7.99 us

profile of v1, /device:TPU:0, one launch (start us, length us, event | category | flops | bytes accessed | tf_op | source)
XLA Modules:
  0.0 240.8 jit_solution(2255577006043613264)
XLA Ops:
  0.6 223.6 %whole.1 = (bf16[24,4,2,32,512]{4,3,2,1,0:T(8,128)(2,1)}, f32[8,256,512]{2,1,0:T(8,128)}, bf16[8,256,512]{2,1,0:T(8,128)(2,1)}, bf16[2048,2048]{1,0:T(8,128)(2,1)}, f32[8,512]{1,0:T(8,128)}, /*index=5*/f32[8,512]{1,0:T(8,128)}) custom-call(bf16[8,256,512]{2,1,0:T(8,128)(2,1)} %tokens.1, bf16[3,2048,512]{2,1,0:T(8,128)(2,1)} %weights.1, ...), custom_call_target="tpu_custom_call" | custom-call | tf_op jit(solution)/shard_map/whole/pallas_call | solution.py:802
  224.3 0.0 copy-start
  224.3 2.8 %copy-done = bf16[24,4,2,32,512]{4,3,2,1,0:T(8,128)(2,1)S(1)} copy-done((bf16[24,4,2,32,512]{4,3,2,1,0:T(8,128)(2,1)S(1)}, bf16[24,4,2,32,512]{4,3,2,1,0:T(8,128)(2,1)}, u32[]{:S(2)}) %copy-start) | copy-done | bytes 6291480
  227.1 0.0 copy-start.1
  227.1 2.2 copy-done.1
  229.3 0.0 copy-start.2
  229.3 1.6 copy-done.2
  230.9 0.0 copy-start.3
  230.9 0.7 copy-done.3
  231.6 0.0 copy-start.4
  231.6 0.7 copy-done.4
  232.3 8.5 %tail.1 = (f32[6144,512]{1,0:T(8,128)}, f32[8,256,512]{2,1,0:T(8,128)}, bf16[8,256,512]{2,1,0:T(8,128)(2,1)}, f32[8,512]{1,0:T(8,128)}, f32[1,512]{1,0:T(1,128)}...) custom-call(bf16[6144,512]{1,0:T(8,128)(2,1)S(1)} %bitcast.14, ...), custom_call_target="tpu_custom_call" | custom-call | tf_op jit(solution)/shard_map/tail/pallas_call | solution.py:905
Async XLA Ops:
  224.3 2.8 %copy-start = (bf16[24,4,2,32,512]{4,3,2,1,0:T(8,128)(2,1)S(1)}, bf16[24,4,2,32,512]{4,3,2,1,0:T(8,128)(2,1)}, u32[]{:S(2)}) copy-start(bf16[24,4,2,32,512]{4,3,2,1,0:T(8,128)(2,1)} %get-tuple-element.25) | copy-start | bytes 18874372
  227.1 2.2 copy-start.1
  229.3 1.6 copy-start.2
  230.9 0.7 copy-start.3
  231.6 0.7 copy-start.4

commit v2 on v1

--- a/solution.py
+++ b/solution.py
@@ -11,7 +11,9 @@
 LANE = 128
 UNIT = 256
 LAG = 2
-SLICE = 7
+PAIR = 80
+LINE = 48
+SENDS = 4
 VMEM_BYTES = 63 << 20
 TAIL = 12
 LATER = 4
@@ -37,17 +39,17 @@
 
 
 def ring_of(tm_count):
-    return 12 if tm_count <= 8 else 3
+    return 14 if tm_count <= 8 else 3
 
 
 def layer_kernel(
     tokens, weights, cotangent, gain, shift, mix_f, mix_r, bias_f, bias_r, bank, selector, resets,
     fin, in_grad, act, low_t, final, totals,
     raw, rx, low, low_t_buf, w_buf, cand, forget, gate, masked, own_tok, cot_raw, cot, mean, inv, keep_mask, grad_buf,
-    act_buf, side, terms, out_buf, row_rx, more, sum_rx, mean_s, inv_s, part_s, entry, fore, back, flow, reset_rows,
+    act_buf, side, terms, out_buf, row_rx, more, sum_rx, mean_s, inv_s, part_s, entry, near, far, flow, reset_rows,
     x_send, x_recv, s_send, s_recv, d_send, d_recv, own_sem, w_sem, cot_sem, act_sem, tr_sem, low_sem,
-    fore_send, fore_recv, back_send, back_recv, ready_sem, out_sem, loc_sem, pair_send, pair_recv, red_send, red_recv,
-    bc_send, bc_recv, swap_send, swap_recv, give_send, give_recv, sib_send, sib_recv, acr_send, acr_recv, row_send,
+    near_send, near_recv, far_send, far_recv, last_send, last_recv, ready_sem, out_sem, loc_sem, pair_send, red_send,
+    bc_send, bc_recv, swap_send, give_send, give_recv, rx_recv, sib_send, sib_recv, acr_send, acr_recv, row_send,
     row_recv, sum_send, sum_recv,
 ):
     rows, steps, width = tokens.shape
@@ -63,7 +65,6 @@
     blocks = CHUNK // BLOCK
     units = 3 * full // UNIT
     per_gate = full // UNIT
-    pieces = UNIT // 4 // CHUNK
 
     def remote(src, dst, send, recv, target):
         return pltpu.make_async_remote_copy(src, dst, send, recv, device_id=target, device_id_type=MESH)
@@ -87,7 +88,7 @@
         return tokens.at[:, pl.ds(pl.multiple_of(ch * CHUNK, CHUNK), CHUNK), :]
 
     def raw_at(ch, block):
-        return raw.at[pl.ds(pl.multiple_of((ch * chan_count + block) * rows, rows), rows)]
+        return raw.at[pl.ds(pl.multiple_of((ch * chan_count + block) * span, span), span)].reshape(rows, CHUNK, width)
 
     def own_copy(ch):
         return pltpu.make_async_copy(piece(ch), raw_at(ch, chan), own_sem.at[ch])
@@ -197,19 +198,24 @@
         s_copy(ch).wait_recv()
         d_copy(ch).wait_recv()
 
-        first = pl.multiple_of(ch * chan_count * rows, rows)
+        first = pl.multiple_of(ch * chan_count * span, span)
+
+        def tokens_at(block, r, t0, cols):
+            at = pl.multiple_of(first + block * span + r * CHUNK + t0, BLOCK)
+            return raw[pl.ds(at, BLOCK), cols].astype(F32)
 
         def each(i, turn):
             r, h = i // blocks, lax.rem(i, blocks)
-            t0 = pl.multiple_of(h * BLOCK, BLOCK)
-            total = jnp.zeros((BLOCK, LANE), F32)
-            for b in range(chan_count):
-                for j in range(tiles):
-                    total = total + turn(raw[first + b * rows + r, pl.ds(t0, BLOCK), lanes(j)].astype(F32), h, r)
-            part_s[h, r] = total
+            totals = [jnp.zeros((BLOCK, LANE), F32) for _ in range(chan_count)]
+            for j in range(tiles):
+                for b in range(chan_count):
+                    totals[b] = totals[b] + turn(tokens_at(b, r, h * BLOCK, lanes(j)))
+            while len(totals) > 1:
+                totals = [a + b for a, b in zip(totals[::2], totals[1::2])]
+            part_s[h, r] = totals[0]
 
         def sum_rows(i, carry):
-            each(i, lambda v, h, r: v)
+            each(i, lambda v: v)
             return carry
 
         lax.fori_loop(0, rows * blocks, sum_rows, 0)
@@ -218,7 +224,7 @@
         def square_rows(i, carry):
             r, h = i // blocks, lax.rem(i, blocks)
             m = mean_s[h, r]
-            each(i, lambda v, h, r: (v - m) * (v - m))
+            each(i, lambda v: (v - m) * (v - m))
             return carry
 
         lax.fori_loop(0, rows * blocks, square_rows, 0)
@@ -231,9 +237,8 @@
 
             def normalize(j, carry, h=h, mean_h=mean_h, inv_h=inv_h):
                 cols = pl.ds(pl.multiple_of(j * LANE, LANE), LANE)
-                where = pl.ds(first + (j // tiles) * rows, rows)
                 inner = pl.ds(pl.multiple_of(lax.rem(j, tiles) * LANE, LANE), LANE)
-                v = raw[where, h * BLOCK : (h + 1) * BLOCK, inner].astype(F32).reshape(part, LANE)
+                v = jnp.concatenate([tokens_at(j // tiles, r, h * BLOCK, inner) for r in range(rows)], axis=0)
                 v = (v - mean_h) * inv_h * gain[0:1, cols] + shift[0:1, cols]
                 low[slot, h * part : (h + 1) * part, cols] = swapped(v, rows, BLOCK).astype(BF16)
                 return carry
@@ -243,8 +248,8 @@
             mean[at, :] = swapped(mean_h, rows, BLOCK)
             inv[at, :] = swapped(inv_h, rows, BLOCK)
             for j in range(tiles):
-                v = raw[pl.ds(first + chan * rows, rows), h * BLOCK : (h + 1) * BLOCK, lanes(j)]
-                own_tok[at, lanes(j)] = swapped(v.astype(F32).reshape(part, LANE), rows, BLOCK).astype(BF16)
+                v = jnp.concatenate([tokens_at(chan, r, h * BLOCK, lanes(j)) for r in range(rows)], axis=0)
+                own_tok[at, lanes(j)] = swapped(v, rows, BLOCK).astype(BF16)
 
         at = pl.ds(base, span)
 
@@ -282,15 +287,22 @@
     zeros = tuple(jnp.zeros((rows, LANE), F32) for _ in range(tiles))
     a_run, b_run = lax.fori_loop(0, chunks, gather_step, (ones, zeros))
 
-    for j in range(tiles):
-        fore[tm, 0, :, lanes(j)] = a_run[j]
-        fore[tm, 1, :, lanes(j)] = b_run[j]
-
-    def fore_copy(source, target):
-        return remote(fore.at[source], fore.at[source], fore_send.at[target], fore_recv.at[source], (target, chan))
-
-    def back_copy(source, target):
-        return remote(back.at[source], back.at[source], back_send.at[target], back_recv.at[source], (target, chan))
+    spans = jnp.where(reset_rows[0] >= tm_count * steps, 1.0, 0.0)
+    last_tm = tm_count - 1
+
+    def spanning(v):
+        return jnp.sum(v * spans, axis=0, keepdims=True)
+
+    def near_copy(way, target):
+        return remote(near.at[way, 0], near.at[way, 1], near_send.at[way], near_recv.at[way], (target, chan))
+
+    def far_copy(way, source, target):
+        return remote(
+            far.at[way, source], far.at[way, source], far_send.at[way, target], far_recv.at[way, source], (target, chan)
+        )
+
+    def last_copy(target):
+        return remote(near.at[0, 0], near.at[0, 2], last_send.at[target], last_recv, (target, chan))
 
     def sum_copy(source, target):
         return remote(sum_rx.at[source], sum_rx.at[source], sum_send.at[target], sum_recv.at[source], (target, chan))
@@ -302,17 +314,29 @@
 
         lax.fori_loop(1, tm_count, one, 0)
 
-    peers(lambda p: fore_copy(tm, p).start())
+    for j in range(tiles):
+        near[0, 0, :, lanes(j)] = b_run[j]
+        far[0, tm, j : j + 1, :] = spanning(a_run[j])
+        far[0, tm, tiles + j : tiles + j + 1, :] = spanning(b_run[j])
+    pl.when(tm < last_tm)(lambda: near_copy(0, tm + 1).start())
+    peers(lambda p: far_copy(0, tm, p).start())
+    pl.when(tm == last_tm)(lambda: peers(lambda p: last_copy(p).start()))
     flip(chunks - 1)
-    peers(lambda p: fore_copy(p, tm).wait_recv())
+    peers(lambda p: far_copy(0, p, tm).wait_recv())
+    pl.when(tm > 0)(lambda: near_copy(0, tm).wait_recv())
 
     def carry_on(d, carry):
         state, here = carry
         here = jnp.where(d == tm, state, here)
-        return fore[d, 0] * state + fore[d, 1], here
-
-    last, here = lax.fori_loop(0, tm_count, carry_on, (entry[...], entry[...]))
-    final[...] = last
+        return far[0, d, 0:tiles, :] * state + far[0, d, tiles : 2 * tiles, :], here
+
+    lead = jnp.concatenate([spanning(entry[:, lanes(j)]) for j in range(tiles)], axis=0)
+    last, here = lax.fori_loop(0, tm_count, carry_on, (lead, lead))
+    states = []
+    for j in range(tiles):
+        row = jnp.broadcast_to(here[j : j + 1], (rows, LANE))
+        others = jnp.where(tm == 0, entry[:, lanes(j)], near[0, 1, :, lanes(j)])
+        states.append(jnp.where(spans > 0, row, others))
     tr_copy(chunks - 1).wait()
     low_copy(0).start()
 
@@ -340,7 +364,7 @@
             grad_buf[2, at, cols] = (gate_grad * o * (1.0 - o)).astype(BF16)
         return tuple(states)
 
-    lax.fori_loop(0, steps // BLOCK, forward, tuple(here[:, lanes(j)] for j in range(tiles)))
+    lax.fori_loop(0, steps // BLOCK, forward, tuple(states))
 
     def start_later():
         flow[0] = jnp.ones((rows, width), F32)
@@ -389,8 +413,11 @@
         return carry
 
     def end_later():
-        back[tm] = flow[1]
-        peers(lambda p: back_copy(tm, p).start())
+        near[1, 0] = flow[1]
+        for j in range(tiles):
+            far[1, tm, j : j + 1, :] = spanning(flow[1, :, lanes(j)])
+        pl.when(tm > 0)(lambda: near_copy(1, tm - 1).start())
+        peers(lambda p: far_copy(1, tm, p).start())
         for target in (sibling, across):
             pl.semaphore_signal(ready_sem, inc=1, device_id=(tm, target), device_id_type=MESH)
         for i in range(2):
@@ -406,120 +433,146 @@
 
     n = tm_count // 2
     o, y = tm // 2, lax.rem(tm, 2)
-    hops = n // 2
     partner = (o * 2 + 1 - y, chan)
     left = ((o - 1) * 2 + y, chan)
     right = ((o + 1) * 2 + y, chan)
-    depth = LAG * (2 * hops + 2)
     ring = ring_of(tm_count)
+    ends, middle = (0, n - 1), (n // 2 - 1, n // 2)
+    lines = [(0, middle[0] + y, n // 2, 1, None)]
+    for l in (1, 2):
+        if n == 4:
+            lines += [(l, ends[l - 1], n - 1, 0, 0), (l, middle[l - 1], n // 2, 0, 1)]
+        else:
+            lines += [(l, middle[l - 1], n // 2, 0, None)]
+    give_stage = 2 * (n // 2) + 2
+    depth = LAG * max([give_stage] + [first + reach + (l > 0) + reach for l, c, reach, first, parity in lines])
     space = -(-depth // ring)
-    lines = [(y, n // 2 - 1 + y, 1), (2, n // 2 - 1, 0), (3, n // 2, 0)]
-
-    def stage(s, number):
+
+    def stage(s, number, parity=None):
         v = s - LAG * number
-        if space == 1:
-            return v, both(v >= 0, v < units)
-        return v // space, both(v >= 0, lax.rem(v, space) == 0, v // space < units)
+        u = v if space == 1 else v // space
+        go = both(v >= 0, u < units)
+        if space > 1:
+            go = both(go, lax.rem(v, space) == 0)
+        return u, go if parity is None else both(go, lax.rem(u, 2) == parity)
 
     def gate_of(u):
         return lax.rem(u // per_gate + 2, 3)
 
-    def fin_at(u, p):
-        return fin.at[gate_of(u) * per_gate + lax.rem(u, per_gate), p]
-
-    def wg_rows(u, p):
-        return pl.ds((u * 4 + p) * pieces, pieces)
-
-    def wg_at(u, p):
-        return raw.at[wg_rows(u, p)]
-
-    def rx_rows(u, place):
-        return pl.ds((lax.rem(u, ring) * SLICE + place) * pieces, pieces)
-
-    def rx_at(u, place):
-        return rx.at[rx_rows(u, place)]
-
-    def arrival(l, column, way):
+    def piece_of(l, mate=False):
+        if l == 0:
+            return (1 - y if mate else y) * PAIR, PAIR
+        return 2 * PAIR + (l - 1) * LINE, LINE
+
+    def wg_rows(l, u, mate=False):
+        start, size = piece_of(l, mate)
+        return pl.ds(pl.multiple_of(u * UNIT + start, 16), size)
+
+    def fin_at(l, u):
+        start, size = piece_of(l)
+        return fin.at[pl.ds(pl.multiple_of((gate_of(u) * per_gate + lax.rem(u, per_gate)) * UNIT + start, 16), size)]
+
+    def rx_rows(u, place, l):
+        start = place * PAIR if l == 0 else 3 * PAIR + (place - 3) * LINE
+        size = PAIR if l == 0 else LINE
+        return pl.ds(pl.multiple_of(lax.rem(u, ring) * (3 * PAIR + 4 * LINE) + start, 16), size)
+
+    def arrival(l, c, column, way, u):
         if l == 0:
             return 1 + way
-        other = 6 if l == 1 else jnp.where(column == lines[1][1], 6, 3)
-        return jnp.where(column == lines[l][1], 3 + way, other)
+        if l == 1:
+            other = 6
+        elif n == 4:
+            other = jnp.where(column == jnp.where(lax.rem(u, 2) == 0, ends[0], middle[0]), 6, 3)
+        else:
+            other = jnp.where(column == middle[0], 6, 3)
+        return jnp.where(column == c, 3 + way, other)
+
+    def launch(make, u):
+        @pl.when(u >= SENDS)
+        def _():
+            make(u - SENDS).wait_send()
+
+        make(u).start()
+
+    def to_rx(src, u, place, l, sem, target):
+        return remote(src, rx.at[rx_rows(u, place, l)], sem, rx_recv.at[lax.rem(u, ring), place], target)
 
     def pair_copy(u):
-        return remote(wg_at(u, 1 - y), rx_at(u, 0), pair_send.at[u], pair_recv.at[u], partner)
-
-    def red_copy(l, u, to_right):
+        return to_rx(raw.at[wg_rows(0, u, True)], u, 0, 0, pair_send.at[lax.rem(u, SENDS)], partner)
+
+    def red_copy(l, c, u, to_right):
         way, column = (0, o + 1) if to_right else (1, o - 1)
-        return remote(
-            wg_at(u, lines[l][0]), rx_at(u, arrival(l, column, way)), red_send.at[l, u], red_recv.at[l, u, way],
+        return to_rx(
+            raw.at[wg_rows(l, u)], u, arrival(l, c, column, way, u), l, red_send.at[l, lax.rem(u, SENDS)],
             right if to_right else left,
         )
 
-    def red_wait(l, u, way):
-        place = arrival(l, o, way)
-        remote(rx_at(u, place), rx_at(u, place), red_send.at[l, u], red_recv.at[l, u, way], partner).wait_recv()
-        return rx[rx_rows(u, place)].astype(F32)
+    def red_wait(l, c, u, way):
+        place = arrival(l, c, o, way, u)
+        at = rx_rows(u, place, l)
+        to_rx(rx.at[at], u, place, l, red_send.at[l, 0], partner).wait_recv()
+        return rx[at].astype(F32)
 
     def bc_copy(l, u, to_right, src):
         return remote(
-            src, fin_at(u, lines[l][0]), bc_send.at[l, u, 1 if to_right else 0], bc_recv.at[l, u],
+            src, fin_at(l, u), bc_send.at[l, lax.rem(u, SENDS), 1 if to_right else 0], bc_recv.at[l, lax.rem(u, ring)],
             right if to_right else left,
         )
 
     def swap_copy(l, u):
-        return remote(wg_at(u, lines[l][0]), rx_at(u, 5), swap_send.at[l - 1, u], swap_recv.at[l - 1, u], partner)
+        return to_rx(raw.at[wg_rows(l, u)], u, 5, l, swap_send.at[lax.rem(u, SENDS)], partner)
 
     def give_copy(u, src):
-        return remote(src, fin_at(u, y), give_send.at[u], give_recv.at[u], partner)
+        return remote(src, fin_at(0, u), give_send.at[lax.rem(u, SENDS)], give_recv.at[lax.rem(u, ring)], partner)
 
     def local_copy(l, u):
-        return pltpu.make_async_copy(wg_at(u, lines[l][0]), fin_at(u, lines[l][0]), loc_sem.at[l, u])
+        return pltpu.make_async_copy(raw.at[wg_rows(l, u)], fin_at(l, u), loc_sem.at[l, lax.rem(u, SENDS)])
 
     def add_to(l, u, *others):
-        at = wg_rows(u, lines[l][0])
+        at = wg_rows(l, u)
         total = raw[at].astype(F32)
         for v in others:
             total = total + v
         raw[at] = total.astype(BF16)
 
-    def red_start(l, u):
-        c = lines[l][1]
-        pl.when(o < c)(lambda: red_copy(l, u, True).start())
-        pl.when(o > c)(lambda: red_copy(l, u, False).start())
+    def red_start(l, c, u):
+        pl.when(o < c)(lambda: launch(lambda v: red_copy(l, c, v, True), u))
+        pl.when(o > c)(lambda: launch(lambda v: red_copy(l, c, v, False), u))
 
     def publish(l, u):
-        src = wg_at(u, lines[l][0])
+        @pl.when(u >= SENDS)
+        def _():
+            local_copy(l, u - SENDS).wait()
+
         local_copy(l, u).start()
-        pl.when(o > 0)(lambda: bc_copy(l, u, False, src).start())
-        pl.when(o < n - 1)(lambda: bc_copy(l, u, True, src).start())
+        pl.when(o > 0)(lambda: launch(lambda v: bc_copy(l, v, False, raw.at[wg_rows(l, v)]), u))
+        pl.when(o < n - 1)(lambda: launch(lambda v: bc_copy(l, v, True, raw.at[wg_rows(l, v)]), u))
         if l == 0:
-            give_copy(u, src).start()
+            launch(lambda v: give_copy(v, raw.at[wg_rows(0, v)]), u)
 
     def block_cols(c):
         return pl.ds(pl.multiple_of(c * width, width), width)
 
     def sib_rows(ch, q):
-        return pl.ds(units * 4 * pieces + (lax.rem(ch, 4) * 2 + q) * rows, rows)
+        return pl.ds(pl.multiple_of(units * UNIT + (lax.rem(ch, 4) * 2 + q) * span, span), span)
 
     def sib_copy(ch, q):
         slot = lax.rem(ch, 2)
         cols = sibling if q == 0 else lax.rem(sibling + 2, 4)
         return remote(
-            terms.at[slot, cols], raw.at[sib_rows(ch, q)], sib_send.at[ch, q], sib_recv.at[ch, q], (tm, sibling)
+            terms.at[slot, cols], raw.at[sib_rows(ch, q)], sib_send.at[q], sib_recv.at[lax.rem(ch, 4), q], (tm, sibling)
         )
 
     def acr_copy(ch):
         return remote(
-            terms.at[lax.rem(ch, 2), across], cot_view(ch), acr_send.at[ch], acr_recv.at[ch], (tm, across)
+            terms.at[lax.rem(ch, 2), across], cot.at[rows_of(ch)], acr_send.at[lax.rem(ch, 2)], acr_recv.at[ch], (tm, across)
         )
-
-    def cot_view(ch):
-        return cot.at[rows_of(ch)].reshape(rows, CHUNK, width)
 
     def row_copy(ch, source, d):
         return remote(
-            row_rx.at[ch, source], row_rx.at[ch, source], row_send.at[ch, d - 1], row_recv.at[ch, source],
-            (tm, lax.rem(chan + d, 4)),
+            row_rx.at[ch, source], row_rx.at[ch, source], row_send.at[lax.rem(ch, 4), d - 1],
+            row_recv.at[lax.rem(ch, 4), source], (tm, lax.rem(chan + d, 4)),
         )
 
     def out_copy(ch):
@@ -545,7 +598,7 @@
                     grad_buf[k, at, :], w_buf[k, b * width : (b + 1) * width, :], (((1,), (1,)), ((), ())),
                     preferred_element_type=F32,
                 )
-            terms[slot, b] = total.astype(BF16).reshape(rows, CHUNK, width)
+            terms[slot, b] = total.astype(BF16)
         sib_copy(ch, 0).start()
         sib_copy(ch, 1).start()
 
@@ -557,7 +610,7 @@
         terms[slot, across] = there.astype(BF16)
         acr_copy(ch).start()
         here = terms[slot, chan].astype(F32) + raw[sib_rows(ch, 0)].astype(F32)
-        cand[rows_of(ch), :] = here.reshape(span, width)
+        cand[rows_of(ch), :] = here
         for q in range(2):
             sib_copy(ch, q).wait_send()
 
@@ -582,6 +635,7 @@
                     total = total + lax.dot_general(lead, p, (((1,), (1,)), ((), ())), preferred_element_type=F32)
         row_rx[ch, chan] = total
         for d in range(1, 4):
+            pl.when(ch >= 4)(lambda d=d: row_copy(ch - 4, chan, d).wait_send())
             row_copy(ch, chan, d).start()
 
     def finish(ch):
@@ -611,13 +665,18 @@
         peers(lambda p: sum_copy(tm, p).start())
 
     def start_backward():
-        peers(lambda p: back_copy(p, tm).wait_recv())
+        peers(lambda p: far_copy(1, p, tm).wait_recv())
+        pl.when(tm < last_tm)(lambda: near_copy(1, tm).wait_recv())
 
         def carry_back(i, v):
             d = tm_count - 1 - i
-            return jnp.where(d > tm, fore[d, 0] * v + back[d], v)
-
-        flow[0] = lax.fori_loop(0, tm_count, carry_back, jnp.zeros((rows, width), F32))
+            return jnp.where(d > tm, far[0, d, 0:tiles, :] * v + far[1, d, 0:tiles, :], v)
+
+        inflow = lax.fori_loop(0, tm_count, carry_back, jnp.zeros((tiles, LANE), F32))
+        for j in range(tiles):
+            row = jnp.broadcast_to(inflow[j : j + 1], (rows, LANE))
+            others = jnp.where(tm == last_tm, 0.0, near[1, 1, :, lanes(j)])
+            flow[0, :, lanes(j)] = jnp.where(spans > 0, row, others)
         flow[1] = jnp.zeros((rows, width), F32)
         flow[2] = jnp.zeros((rows, width), F32)
 
@@ -646,66 +705,67 @@
         return carry
 
     def slot_step(s, carry):
-        u, go = stage(s, 2 * hops + 2)
-        pl.when(go)(lambda: give_copy(u, wg_at(u, 0)).wait_recv())
-
-        for l in range(3):
-            p, c, first = lines[l]
-            late = first + hops + (0 if l == 0 else 1)
-            u, go = stage(s, late + jnp.abs(o - c))
+        u, go = stage(s, give_stage)
+        pl.when(go)(lambda: give_copy(u, raw.at[wg_rows(0, u)]).wait_recv())
+
+        for l, c, reach, first, parity in lines:
+            late = first + reach + (1 if l else 0)
+            u, go = stage(s, late + jnp.abs(o - c), parity)
 
             @pl.when(both(o != c, go))
             def _(l=l, c=c, u=u):
-                here = fin_at(u, lines[l][0])
-                bc_copy(l, u, True, here).wait_recv()
-                pl.when(both(o < c, o > 0))(lambda: bc_copy(l, u, False, here).start())
-                pl.when(both(o > c, o < n - 1))(lambda: bc_copy(l, u, True, here).start())
+                bc_copy(l, u, True, fin_at(l, u)).wait_recv()
+                pl.when(both(o < c, o > 0))(lambda: launch(lambda v: bc_copy(l, v, False, fin_at(l, v)), u))
+                pl.when(both(o > c, o < n - 1))(lambda: launch(lambda v: bc_copy(l, v, True, fin_at(l, v)), u))
                 if l == 0:
-                    give_copy(u, here).start()
-
-            if l > 0:
-                u, go = stage(s, late)
-
-                @pl.when(both(o == c, go))
-                def _(l=l, u=u):
-                    swap_copy(l, u).wait()
-                    add_to(l, u, rx[rx_rows(u, 5)].astype(F32))
-                    publish(l, u)
-
-            u, go = stage(s, first + hops)
+                    launch(lambda v: give_copy(v, fin_at(0, v)), u)
+
+        for l, c, reach, first, parity in lines[1:]:
+            u, go = stage(s, reach + 1, parity)
 
             @pl.when(both(o == c, go))
             def _(l=l, u=u):
-                if n > 2:
-                    add_to(l, u, red_wait(l, u, 0), red_wait(l, u, 1))
+                swap_copy(l, u).wait()
+                add_to(l, u, rx[rx_rows(u, 5, l)].astype(F32))
+                publish(l, u)
+
+        for l, c, reach, first, parity in lines:
+            u, go = stage(s, first + reach, parity)
+
+            @pl.when(both(o == c, go))
+            def _(l=l, c=c, u=u):
+                if l == 0 and n > 2:
+                    add_to(l, u, red_wait(l, c, u, 0), red_wait(l, c, u, 1))
+                elif l > 0 and 0 < c < n - 1:
+                    add_to(l, u, red_wait(l, c, u, 0), red_wait(l, c, u, 1))
                 else:
-                    pl.when(o > 0)(lambda: add_to(l, u, red_wait(l, u, 0)))
-                    pl.when(o < n - 1)(lambda: add_to(l, u, red_wait(l, u, 1)))
+                    pl.when(o > 0)(lambda: add_to(l, u, red_wait(l, c, u, 0)))
+                    pl.when(o < n - 1)(lambda: add_to(l, u, red_wait(l, c, u, 1)))
                 if l == 0:
                     publish(l, u)
                 else:
                     swap_copy(l, u).start()
 
-            hop = jnp.where(o < c, o, n - 1 - o)
-            u, go = stage(s, first + hop)
+        for l, c, reach, first, parity in lines:
+            u, go = stage(s, first + jnp.where(o < c, o, n - 1 - o), parity)
 
             @pl.when(both(o < c, o > 0, go))
-            def _(l=l, u=u):
-                add_to(l, u, red_wait(l, u, 0))
-                red_copy(l, u, True).start()
+            def _(l=l, c=c, u=u):
+                add_to(l, u, red_wait(l, c, u, 0))
+                launch(lambda v: red_copy(l, c, v, True), u)
 
             @pl.when(both(o > c, o < n - 1, go))
-            def _(l=l, u=u):
-                add_to(l, u, red_wait(l, u, 1))
-                red_copy(l, u, False).start()
+            def _(l=l, c=c, u=u):
+                add_to(l, u, red_wait(l, c, u, 1))
+                launch(lambda v: red_copy(l, c, v, False), u)
 
         u, go = stage(s, 1)
 
         @pl.when(go)
         def _():
             pair_copy(u).wait_recv()
-            add_to(0, u, rx[rx_rows(u, 0)].astype(F32))
-            pl.when(jnp.logical_or(o == 0, o == n - 1))(lambda: red_start(0, u))
+            add_to(0, u, rx[rx_rows(u, 0, 0)].astype(F32))
+            pl.when(jnp.logical_or(o == 0, o == n - 1))(lambda: red_start(0, lines[0][1], u))
 
         u0, go0 = stage(s, 0)
 
@@ -713,14 +773,14 @@
         def _():
             pl.when(u0 + 1 < units)(lambda: low_copy(u0 + 1).start())
             low_copy(u0).wait()
-            g = jnp.dot(low[lax.rem(u0, 2)], grad_buf[gate_of(u0)], preferred_element_type=F32).astype(BF16)
-            raw[pl.ds(u0 * 4 * pieces, 4 * pieces)] = g.reshape(4 * pieces, CHUNK, width)
-            pair_copy(u0).start()
-
-            @pl.when(jnp.logical_or(o == 0, o == n - 1))
-            def _():
-                red_start(1, u0)
-                red_start(2, u0)
+            g = jnp.dot(low[lax.rem(u0, 2)], grad_buf[gate_of(u0)], preferred_element_type=F32)
+            raw[pl.ds(pl.multiple_of(u0 * UNIT, UNIT), UNIT)] = g.astype(BF16)
+            launch(pair_copy, u0)
+            for l, c, reach, first, parity in lines[1:]:
+                mine_now = jnp.logical_or(o == 0, o == n - 1)
+                if parity is not None:
+                    mine_now = both(mine_now, lax.rem(u0, 2) == parity)
+                pl.when(mine_now)(lambda l=l, c=c: red_start(l, c, u0))
 
         count = steps // BLOCK
         pl.when(s == 0)(start_later)
@@ -750,24 +810,31 @@
     lax.fori_loop(0, slots, slot_step, 0)
 
     def close_unit(u, carry):
-        give_copy(u, wg_at(u, 0)).wait_send()
+        give_copy(u, raw.at[wg_rows(0, u)]).wait_send()
         pair_copy(u).wait_send()
-        for l in range(3):
-            c = lines[l][1]
-            src = wg_at(u, 0)
-            pl.when(o != c)(lambda l=l: red_copy(l, u, True).wait_send())
-            pl.when(o == c)(lambda l=l: local_copy(l, u).wait())
-            pl.when(both(o <= c, o > 0))(lambda l=l: bc_copy(l, u, False, src).wait_send())
-            pl.when(both(o >= c, o < n - 1))(lambda l=l: bc_copy(l, u, True, src).wait_send())
+        for l, c, reach, first, parity in lines:
+
+            @pl.when(True if parity is None else lax.rem(u, 2) == parity)
+            def _(l=l, c=c):
+                src = raw.at[wg_rows(l, u)]
+                pl.when(o != c)(lambda: red_copy(l, c, u, True).wait_send())
+                pl.when(o == c)(lambda: local_copy(l, u).wait())
+                pl.when(both(o <= c, o > 0))(lambda: bc_copy(l, u, False, src).wait_send())
+                pl.when(both(o >= c, o < n - 1))(lambda: bc_copy(l, u, True, src).wait_send())
+
         return carry
 
-    lax.fori_loop(0, units, close_unit, 0)
+    lax.fori_loop(units - SENDS, units, close_unit, 0)
 
     def close_chunk(ch, carry):
         x_copy(ch).wait_send()
         s_copy(ch).wait_send()
-        for d in range(1, 4):
-            row_copy(ch, chan, d).wait_send()
+
+        @pl.when(ch >= chunks - 4)
+        def _():
+            for d in range(1, 4):
+                row_copy(ch, chan, d).wait_send()
+
         return carry
 
     lax.fori_loop(0, chunks, close_chunk, 0)
@@ -775,8 +842,16 @@
         out_copy(ch).wait()
         act_copy(ch).wait()
         acr_copy(ch).wait_send()
-    peers(lambda p: fore_copy(tm, p).wait_send())
-    peers(lambda p: back_copy(tm, p).wait_send())
+    for way in range(2):
+        peers(lambda p, way=way: far_copy(way, tm, p).wait_send())
+    pl.when(tm < last_tm)(lambda: near_copy(0, tm).wait_send())
+    pl.when(tm > 0)(lambda: near_copy(1, tm).wait_send())
+    pl.when(tm == last_tm)(lambda: peers(lambda p: last_copy(p).wait_send()))
+    pl.when(tm != last_tm)(lambda: last_copy(tm).wait_recv())
+    for j in range(tiles):
+        row = jnp.broadcast_to(last[j : j + 1], (rows, LANE))
+        others = jnp.where(tm == last_tm, near[0, 0, :, lanes(j)], near[0, 2, :, lanes(j)])
+        final[:, lanes(j)] = jnp.where(spans > 0, row, others)
     peers(lambda p: sum_copy(p, tm).wait_recv())
     peers(lambda p: sum_copy(tm, p).wait_send())
     totals[...] = lax.fori_loop(0, tm_count, lambda d, v: v + sum_rx[d], jnp.zeros(totals.shape, F32))
@@ -790,7 +865,7 @@
     span = CHUNK * rows
     count = steps * rows
     units = 3 * full // UNIT
-    pieces = UNIT // 4 // CHUNK
+    ring = ring_of(tm_count)
     hbm = pl.BlockSpec(memory_space=pl.ANY)
     vmem = pl.BlockSpec(memory_space=pltpu.VMEM)
     smem = pl.BlockSpec(memory_space=pltpu.SMEM)
@@ -802,7 +877,7 @@
     return pl.pallas_call(
         layer_kernel,
         out_shape=(
-            jax.ShapeDtypeStruct((units, 4, pieces, CHUNK, width), BF16),
+            jax.ShapeDtypeStruct((units * UNIT, width), BF16),
             jax.ShapeDtypeStruct(tokens.shape, F32),
             jax.ShapeDtypeStruct(tokens.shape, BF16),
             jax.ShapeDtypeStruct((full, count), BF16),
@@ -812,8 +887,8 @@
         in_specs=[hbm, hbm, hbm] + [vmem] * 7 + [smem, vmem],
         out_specs=(hbm, hbm, hbm, hbm, vmem, vmem),
         scratch_shapes=[
-            pltpu.VMEM((chunks * chan_count * rows, CHUNK, width), BF16),
-            pltpu.VMEM((ring_of(tm_count) * SLICE * pieces, CHUNK, width), BF16),
+            pltpu.VMEM((chunks * chan_count * span, width), BF16),
+            pltpu.VMEM((ring * (3 * PAIR + 4 * LINE), width), BF16),
             pltpu.VMEM((2, span, full), BF16),
             pltpu.VMEM((full, span), BF16),
             pltpu.VMEM((3, full, width), BF16),
@@ -825,25 +900,24 @@
             pltpu.VMEM((3, count, width), BF16),
             pltpu.VMEM((2, rows, CHUNK, width), BF16),
             short,
-            pltpu.VMEM((2, chan_count, rows, CHUNK, width), BF16),
+            pltpu.VMEM((2, chan_count, span, width), BF16),
             pltpu.VMEM((2, rows, CHUNK, width), F32),
             pltpu.VMEM((chunks, 4, 8, span), F32),
             pltpu.VMEM((2, rows, width), F32),
             pltpu.VMEM((tm_count, 8, width), F32),
             stat, stat, stat,
             pltpu.VMEM((rows, width), F32),
-            pltpu.VMEM((tm_count, 2, rows, width), F32),
-            pltpu.VMEM((tm_count, rows, width), F32),
+            pltpu.VMEM((2, 3, rows, width), F32),
+            pltpu.VMEM((2, tm_count, 8, LANE), F32),
             pltpu.VMEM((4, rows, width), F32),
             pltpu.VMEM((resets.shape[1], rows, LANE), jnp.int32),
             dma((chunks,)), dma((chunks,)), dma((chunks,)), dma((chunks,)), dma((chunks,)), dma((chunks,)), dma((chunks,)),
             dma((3,)), dma((2,)), dma((2,)), dma(()), dma((2,)),
-            dma((tm_count,)), dma((tm_count,)), dma((tm_count,)), dma((tm_count,)),
+            dma((2,)), dma((2,)), dma((2, tm_count)), dma((2, tm_count)), dma((tm_count,)), dma(()),
             pltpu.SemaphoreType.REGULAR,
-            dma((2,)), dma((3, units)), dma((units,)), dma((units,)),
-            dma((3, units)), dma((3, units, 2)), dma((3, units, 2)), dma((3, units)), dma((2, units)), dma((2, units)),
-            dma((units,)), dma((units,)), dma((chunks, 2)), dma((chunks, 2)), dma((chunks,)), dma((chunks,)),
-            dma((chunks, 3)), dma((chunks, 4)), dma((tm_count,)), dma((tm_count,)),
+            dma((2,)), dma((3, SENDS)), dma((SENDS,)), dma((3, SENDS)), dma((3, SENDS, 2)), dma((3, ring)), dma((SENDS,)),
+            dma((SENDS,)), dma((ring,)), dma((ring, 7)), dma((2,)), dma((4, 2)), dma((2,)), dma((chunks,)),
+            dma((4, 3)), dma((4, 4)), dma((tm_count,)), dma((tm_count,)),
         ],
         compiler_params=pltpu.CompilerParams(collective_id=0, has_side_effects=True, vmem_limit_bytes=VMEM_BYTES),
         name="whole",
@@ -917,7 +991,7 @@
             pltpu.VMEM(in_grad.shape, F32), pltpu.VMEM(act.shape, BF16),
             dma((TAIL,)), dma((TAIL,)), dma((2, rows)), dma((2, rows)),
         ],
-        compiler_params=pltpu.CompilerParams(vmem_limit_bytes=40 << 20),
+        compiler_params=pltpu.CompilerParams(vmem_limit_bytes=VMEM_BYTES),
         name="tail",
     )(flat, in_grad, act, final, totals)
 

time: 241 us -> 218 us (0.905)
  Pallas kernels: 232 us -> 217 us
  local copies, waits for them, and re-layouts: 7.99 us -> 0 us
    pallas_call x1, Pallas kernels: 224 us -> 205 us  [layer(): pl.pallas_call(layer_kernel, out_shape=(jax.ShapeDtypeStruct((units * UNI...]
    unnamed x10 -> x0, local copies, waits for them, and re-layouts: 7.99 us -> none
    pallas_call x1, Pallas kernels: 8.49 us -> 12.7 us  [tail(): pl.pallas_call(tail_kernel, out_shape=(jax.ShapeDtypeStruct(flat.shape, F...]
where the time goes in v2:
time: 218 us
  Pallas kernels  217 us (100%)
    pallas_call x1, Pallas kernels, layer(): pl.pallas_call(layer_kernel, out_shape=(jax.ShapeDtypeStruct((units * UNI...  205 us
    pallas_call x1, Pallas kernels, tail(): pl.pallas_call(tail_kernel, out_shape=(jax.ShapeDtypeStruct(flat.shape, F...  12.7 us

profile of v2, /device:TPU:0, one launch (start us, length us, event | category | flops | bytes accessed | tf_op | source)
XLA Modules:
  0.0 218.1 jit_solution(5277238463150704653)
XLA Ops:
  0.6 204.7 %whole.1 = (bf16[6144,512]{1,0:T(8,128)(2,1)}, f32[8,256,512]{2,1,0:T(8,128)}, bf16[8,256,512]{2,1,0:T(8,128)(2,1)}, bf16[2048,2048]{1,0:T(8,128)(2,1)}, f32[8,512]{1,0:T(8,128)}, /*index=5*/f32[8,512]{1,0:T(8,128)}) custom-call(bf16[8,256,512]{2,1,0:T(8,128)(2,1)} %tokens.1, bf16[3,2048,512]{2,1,0:T(8,128)(2,1)} %weights.1, bf16[8,256,512]{2,1,0:T(8,128)(2,1)} %cotangent.1, ...), custom_call_target="tpu_custom_call" | custom-call | tf_op jit(solution)/shard_map/whole/pallas_call | solution.py:877
  205.3 12.7 %tail.1 = (f32[6144,512]{1,0:T(8,128)}, f32[8,256,512]{2,1,0:T(8,128)}, bf16[8,256,512]{2,1,0:T(8,128)(2,1)}, f32[8,512]{1,0:T(8,128)}, f32[1,512]{1,0:T(1,128)}...) custom-call(bf16[6144,512]{1,0:T(8,128)(2,1)} %get-tuple-element.25.fin, ...), custom_call_target="tpu_custom_call" | custom-call | tf_op jit(solution)/shard_map/tail/pallas_call | solution.py:979

commit v3 on v2

--- a/solution.py
+++ b/solution.py
@@ -15,7 +15,7 @@
 LINE = 48
 SENDS = 4
 VMEM_BYTES = 63 << 20
-TAIL = 12
+TAIL = 4
 LATER = 4
 FIRST = 8
 MESH = pl.DeviceIdType.MESH
@@ -166,7 +166,7 @@
             low_t_buf[cols, :] = jnp.transpose(low[lax.rem(ch, 2), :, cols])
             return carry
 
-        lax.fori_loop(0, full // 256, one, 0)
+        lax.fori_loop(0, full // 256, one, 0, unroll=2)
         tr_copy(ch).start()
 
     def gather_step(ch, carry):
@@ -185,15 +185,14 @@
         base = pl.multiple_of(ch * span, span)
         slot = lax.rem(ch, 2)
 
+        x_copy(ch).wait_recv()
+        d_copy(ch).start()
         cot_copy(ch).wait()
         for h in range(blocks):
             for j in range(tiles):
                 v = cot_raw[slot, :, h * BLOCK : (h + 1) * BLOCK, lanes(j)].astype(F32).reshape(part, LANE)
                 cot[pl.ds(pl.multiple_of(base + h * part, part), part), lanes(j)] = swapped(v, rows, BLOCK).astype(BF16)
         pl.when(ch >= 1)(lambda: flip(ch - 1))
-
-        x_copy(ch).wait_recv()
-        d_copy(ch).start()
         own_copy(ch).wait()
         s_copy(ch).wait_recv()
         d_copy(ch).wait_recv()
@@ -218,7 +217,7 @@
             each(i, lambda v: v)
             return carry
 
-        lax.fori_loop(0, rows * blocks, sum_rows, 0)
+        lax.fori_loop(0, rows * blocks, sum_rows, 0, unroll=2)
         mean_s[...] = jnp.broadcast_to(jnp.sum(part_s[...], axis=-1, keepdims=True) * (1.0 / full), mean_s.shape)
 
         def square_rows(i, carry):
@@ -227,7 +226,7 @@
             each(i, lambda v: (v - m) * (v - m))
             return carry
 
-        lax.fori_loop(0, rows * blocks, square_rows, 0)
+        lax.fori_loop(0, rows * blocks, square_rows, 0, unroll=2)
         var = jnp.sum(part_s[...], axis=-1, keepdims=True) * (1.0 / full)
         inv_s[...] = jnp.broadcast_to(lax.rsqrt(var + EPSILON), inv_s.shape)
 
@@ -243,7 +242,7 @@
                 low[slot, h * part : (h + 1) * part, cols] = swapped(v, rows, BLOCK).astype(BF16)
                 return carry
 
-            lax.fori_loop(0, full // LANE, normalize, 0)
+            lax.fori_loop(0, full // LANE, normalize, 0, unroll=2)
             at = pl.ds(pl.multiple_of(base + h * part, part), part)
             mean[at, :] = swapped(mean_h, rows, BLOCK)
             inv[at, :] = swapped(inv_h, rows, BLOCK)
@@ -746,27 +745,6 @@
                 else:
                     swap_copy(l, u).start()
 
-        for l, c, reach, first, parity in lines:
-            u, go = stage(s, first + jnp.where(o < c, o, n - 1 - o), parity)
-
-            @pl.when(both(o < c, o > 0, go))
-            def _(l=l, c=c, u=u):
-                add_to(l, u, red_wait(l, c, u, 0))
-                launch(lambda v: red_copy(l, c, v, True), u)
-
-            @pl.when(both(o > c, o < n - 1, go))
-            def _(l=l, c=c, u=u):
-                add_to(l, u, red_wait(l, c, u, 1))
-                launch(lambda v: red_copy(l, c, v, False), u)
-
-        u, go = stage(s, 1)
-
-        @pl.when(go)
-        def _():
-            pair_copy(u).wait_recv()
-            add_to(0, u, rx[rx_rows(u, 0, 0)].astype(F32))
-            pl.when(jnp.logical_or(o == 0, o == n - 1))(lambda: red_start(0, lines[0][1], u))
-
         u0, go0 = stage(s, 0)
 
         @pl.when(go0)
@@ -781,6 +759,27 @@
                 if parity is not None:
                     mine_now = both(mine_now, lax.rem(u0, 2) == parity)
                 pl.when(mine_now)(lambda l=l, c=c: red_start(l, c, u0))
+
+        for l, c, reach, first, parity in lines:
+            u, go = stage(s, first + jnp.where(o < c, o, n - 1 - o), parity)
+
+            @pl.when(both(o < c, o > 0, go))
+            def _(l=l, c=c, u=u):
+                add_to(l, u, red_wait(l, c, u, 0))
+                launch(lambda v: red_copy(l, c, v, True), u)
+
+            @pl.when(both(o > c, o < n - 1, go))
+            def _(l=l, c=c, u=u):
+                add_to(l, u, red_wait(l, c, u, 1))
+                launch(lambda v: red_copy(l, c, v, False), u)
+
+        u, go = stage(s, 1)
+
+        @pl.when(go)
+        def _():
+            pair_copy(u).wait_recv()
+            add_to(0, u, rx[rx_rows(u, 0, 0)].astype(F32))
+            pl.when(jnp.logical_or(o == 0, o == n - 1))(lambda: red_start(0, lines[0][1], u))
 
         count = steps // BLOCK
         pl.when(s == 0)(start_later)
@@ -930,7 +929,6 @@
 ):
     parts = fin_sem.shape[0]
     size = fin.shape[0] // parts
-    rows = in_sem.shape[1]
 
     def move(src, dst, sem, i, n):
         at = pl.ds(i * n, n)
@@ -940,28 +938,31 @@
     stores = [move(wide_buf, wide_out, wide_sem.at[i], i, size) for i in range(parts)]
     pairs = []
     for src, buf, dst, sem in ((in_grad, in_buf, in_out, in_sem), (act, act_buf, act_out, act_sem)):
-        for r in range(rows):
-            pairs.append((move(src, buf, sem.at[0, r], r, 1), move(buf, dst, sem.at[1, r], r, 1)))
-    for copy in loads:
-        copy.start()
-    for copy, _ in pairs:
-        copy.start()
+        n = sem.shape[1]
+        some = src.shape[0] // n
+        pairs += [(move(src, buf, sem.at[0, i], i, some), move(buf, dst, sem.at[1, i], i, some)) for i in range(n)]
+    for i in range(max(parts, len(pairs))):
+        if i < parts:
+            loads[i].start()
+        if i < len(pairs):
+            pairs[i][0].start()
     final_out[...] = final[...]
     for i, ref in enumerate((s0, s1, s2, s3, s4, s5)):
         ref[...] = totals[i : i + 1, :]
-    for i in range(parts):
-        loads[i].wait()
-
-        def cast(j, carry, i=i):
-            at = pl.ds(pl.multiple_of(i * size + j * 64, 64), 64)
-            wide_buf[at] = fin_buf[at].astype(F32)
-            return carry
-
-        lax.fori_loop(0, size // 64, cast, 0)
-        stores[i].start()
-    for copy, onward in pairs:
-        copy.wait()
-        onward.start()
+    for i in range(max(parts, len(pairs))):
+        if i < parts:
+            loads[i].wait()
+
+            def cast(j, carry, i=i):
+                at = pl.ds(pl.multiple_of(i * size + j * 64, 64), 64)
+                wide_buf[at] = fin_buf[at].astype(F32)
+                return carry
+
+            lax.fori_loop(0, size // 64, cast, 0, unroll=2)
+            stores[i].start()
+        if i < len(pairs):
+            pairs[i][0].wait()
+            pairs[i][1].start()
     for copy in stores:
         copy.wait()
     for _, onward in pairs:
@@ -971,7 +972,6 @@
 def tail(fin, in_grad, act, final, totals):
     width = fin.shape[-1]
     flat = fin.reshape(-1, width)
-    rows = in_grad.shape[0]
     hbm = pl.BlockSpec(memory_space=pl.ANY)
     vmem = pl.BlockSpec(memory_space=pltpu.VMEM)
     dma = pltpu.SemaphoreType.DMA
@@ -989,7 +989,7 @@
         scratch_shapes=[
             pltpu.VMEM(flat.shape, BF16), pltpu.VMEM(flat.shape, F32),
             pltpu.VMEM(in_grad.shape, F32), pltpu.VMEM(act.shape, BF16),
-            dma((TAIL,)), dma((TAIL,)), dma((2, rows)), dma((2, rows)),
+            dma((TAIL,)), dma((TAIL,)), dma((2, 4)), dma((2, 2)),
         ],
         compiler_params=pltpu.CompilerParams(vmem_limit_bytes=VMEM_BYTES),
         name="tail",

time: 218 us -> 210 us (0.963)
  Pallas kernels: 217 us -> 209 us
    pallas_call x1, Pallas kernels: 205 us -> 197 us  [layer(): pl.pallas_call(layer_kernel, out_shape=(jax.ShapeDtypeStruct((units * UNI...]
where the time goes in v3:
time: 210 us; the launch traced here: 209 us
  Pallas kernels  209 us (100%)
    pallas_call x1, Pallas kernels, layer(): pl.pallas_call(layer_kernel, out_shape=(jax.ShapeDtypeStruct((units * UNI...  197 us
    pallas_call x1, Pallas kernels, tail(): pl.pallas_call(tail_kernel, out_shape=(jax.ShapeDtypeStruct(flat.shape, F...  11.8 us

profile of v3, /device:TPU:0, one launch (start us, length us, event | category | flops | bytes accessed | tf_op | source)
XLA Modules:
  0.0 209.4 jit_solution(1850269452841086775)
XLA Ops:
  0.6 197.0 %whole.1 = (bf16[6144,512]{1,0:T(8,128)(2,1)}, f32[8,256,512]{2,1,0:T(8,128)}, bf16[8,256,512]{2,1,0:T(8,128)(2,1)}, bf16[2048,2048]{1,0:T(8,128)(2,1)}, f32[8,512]{1,0:T(8,128)}, /*index=5*/f32[8,512]{1,0:T(8,128)}) custom-call(bf16[8,256,512]{2,1,0:T(8,128)(2,1)} %tokens.1, bf16[3,2048,512]{2,1,0:T(8,128)(2,1)} %weights.1, bf16[8,256,512]{2,1,0:T(8,128)(2,1)} %cotangent.1, ...), custom_call_target="tpu_custom_call" | custom-call | tf_op jit(solution)/shard_map/whole/pallas_call | solution.py:876
  197.7 11.8 %tail.1 = (f32[6144,512]{1,0:T(8,128)}, f32[8,256,512]{2,1,0:T(8,128)}, bf16[8,256,512]{2,1,0:T(8,128)(2,1)}, f32[8,512]{1,0:T(8,128)}, f32[1,512]{1,0:T(1,128)}...) custom-call(bf16[6144,512]{1,0:T(8,128)(2,1)} %get-tuple-element.25.fin, ...), custom_call_target="tpu_custom_call" | custom-call | tf_op jit(solution)/shard_map/tail/pallas_call | solution.py:979

commit v4 on v3

--- a/solution.py
+++ b/solution.py
@@ -44,10 +44,10 @@
 
 def layer_kernel(
     tokens, weights, cotangent, gain, shift, mix_f, mix_r, bias_f, bias_r, bank, selector, resets,
-    fin, in_grad, act, low_t, final, totals,
-    raw, rx, low, low_t_buf, w_buf, cand, forget, gate, masked, own_tok, cot_raw, cot, mean, inv, keep_mask, grad_buf,
+    fin, in_grad, act, low_all, final, totals,
+    raw, rx, low, left_buf, w_buf, cand, forget, gate, masked, own_tok, cot_raw, cot, mean, inv, keep_mask, grad_buf,
     act_buf, side, terms, out_buf, row_rx, more, sum_rx, mean_s, inv_s, part_s, entry, near, far, flow, reset_rows,
-    x_send, x_recv, s_send, s_recv, d_send, d_recv, own_sem, w_sem, cot_sem, act_sem, tr_sem, low_sem,
+    x_send, x_recv, s_send, s_recv, d_send, d_recv, own_sem, w_sem, cot_sem, act_sem, keep_sem, low_sem,
     near_send, near_recv, far_send, far_recv, last_send, last_recv, ready_sem, out_sem, loc_sem, pair_send, red_send,
     bc_send, bc_recv, swap_send, give_send, give_recv, rx_recv, sib_send, sib_recv, acr_send, acr_recv, row_send,
     row_recv, sum_send, sum_recv,
@@ -84,23 +84,37 @@
     def rows_of(ch):
         return pl.ds(pl.multiple_of(ch * span, span), span)
 
-    def piece(ch):
-        return tokens.at[:, pl.ds(pl.multiple_of(ch * CHUNK, CHUNK), CHUNK), :]
-
-    def raw_at(ch, block):
-        return raw.at[pl.ds(pl.multiple_of((ch * chan_count + block) * span, span), span)].reshape(rows, CHUNK, width)
-
-    def own_copy(ch):
-        return pltpu.make_async_copy(piece(ch), raw_at(ch, chan), own_sem.at[ch])
-
-    def x_copy(ch):
-        return remote(piece(ch), raw_at(ch, chan), x_send.at[ch], x_recv.at[ch], (tm, across))
-
-    def s_copy(ch):
-        return remote(piece(ch), raw_at(ch, chan), s_send.at[ch], s_recv.at[ch], (tm, sibling))
-
-    def d_copy(ch):
-        return remote(raw_at(ch, across), raw_at(ch, across), d_send.at[ch], d_recv.at[ch], (tm, sibling))
+    def raw_rows(ch, block, h0, h1):
+        return pl.ds(pl.multiple_of((ch * chan_count + block) * span + h0 * part, part), (h1 - h0) * part)
+
+    def token_copies(ch, h0, h1, copy):
+        at = [pl.ds(pl.multiple_of(ch * CHUNK + h * BLOCK, BLOCK), BLOCK) for h in range(h0, h1)]
+        return [
+            copy(tokens.at[:, t, :], raw.at[raw_rows(ch, chan, h, h + 1)].reshape(rows, BLOCK, width), ch + h0)
+            for h, t in zip(range(h0, h1), at)
+        ]
+
+    def own_move(src, dst, sem):
+        return pltpu.make_async_copy(src, dst, own_sem.at[sem])
+
+    def x_move(src, dst, sem):
+        return remote(src, dst, x_send.at[sem], x_recv.at[sem], (tm, across))
+
+    def s_move(src, dst, sem):
+        return remote(src, dst, s_send.at[sem], s_recv.at[sem], (tm, sibling))
+
+    def arrived(ch, block, h0, h1, copy):
+        here = raw.at[raw_rows(ch, block, h0, h1)]
+        return copy(here, here, ch + h0)
+
+    def send_tokens(ch, h0, h1):
+        for copy in (own_move, x_move, s_move):
+            for c in token_copies(ch, h0, h1, copy):
+                c.start()
+
+    def d_copy(ch, h0, h1):
+        view = raw.at[raw_rows(ch, across, h0, h1)]
+        return remote(view, view, d_send.at[ch + h0], d_recv.at[ch + h0], (tm, sibling))
 
     def cot_copy(ch):
         at = pl.ds(pl.multiple_of(ch * CHUNK, CHUNK), CHUNK)
@@ -110,12 +124,12 @@
         at = pl.ds(pl.multiple_of(ch * CHUNK, CHUNK), CHUNK)
         return pltpu.make_async_copy(act_buf.at[lax.rem(ch, 2)], act.at[:, at, :], act_sem.at[lax.rem(ch, 2)])
 
-    def tr_copy(ch):
-        return pltpu.make_async_copy(low_t_buf, low_t.at[:, rows_of(ch)], tr_sem)
+    def keep_copy(ch):
+        return pltpu.make_async_copy(low.at[lax.rem(ch, 2)], low_all.at[rows_of(ch)], keep_sem.at[lax.rem(ch, 2)])
 
     def low_copy(u):
         at = pl.ds(pl.multiple_of(lax.rem(u, per_gate) * UNIT, UNIT), UNIT)
-        return pltpu.make_async_copy(low_t.at[at], low.at[lax.rem(u, 2)], low_sem.at[lax.rem(u, 2)])
+        return pltpu.make_async_copy(low_all.at[:, at], left_buf.at[lax.rem(u, 2)], low_sem.at[lax.rem(u, 2)])
 
     w_copies = [pltpu.make_async_copy(weights.at[k], w_buf.at[k], w_sem.at[k]) for k in range(3)]
 
@@ -128,15 +142,16 @@
         return carry
 
     lax.fori_loop(1, tm_count, greet, 0)
-    own_copy(0).start()
-    own_copy(1).start()
+    for ch in range(2):
+        for copy in token_copies(ch, 0, blocks, own_move):
+            copy.start()
     cot_copy(0).start()
     for copy in w_copies:
         copy.start()
     pl.semaphore_wait(barrier, tm_count + 2)
     for ch in range(2):
-        x_copy(ch).start()
-        s_copy(ch).start()
+        for copy in token_copies(ch, 0, blocks, x_move) + token_copies(ch, 0, blocks, s_move):
+            copy.start()
 
     count = resets.shape[1]
     for j in range(count):
@@ -156,59 +171,71 @@
     for r in range(rows):
         entry[r : r + 1, :] = bank[pl.ds(selector[r], 1), :]
 
-    def flip(ch):
-        @pl.when(ch >= 1)
-        def _():
-            tr_copy(ch - 1).wait()
-
-        def one(j, carry):
-            cols = pl.ds(pl.multiple_of(j * 256, 256), 256)
-            low_t_buf[cols, :] = jnp.transpose(low[lax.rem(ch, 2), :, cols])
-            return carry
-
-        lax.fori_loop(0, full // 256, one, 0, unroll=2)
-        tr_copy(ch).start()
-
-    def gather_step(ch, carry):
-        a_run, b_run = carry
-
-        @pl.when(ch + 2 < chunks)
-        def _():
-            own_copy(ch + 2).start()
-            x_copy(ch + 2).start()
-            s_copy(ch + 2).start()
-
-        @pl.when(ch + 1 < chunks)
-        def _():
+    def send_last():
+        for h in range(blocks):
+            send_tokens(chunks - 1, h, h + 1)
+
+    def gates(b, carry):
+        a_list, b_list = list(carry[0]), list(carry[1])
+        at = pl.ds(pl.multiple_of(b * part, part), part)
+        mask = keep_mask[at, :]
+        for j in range(tiles):
+            cols = lanes(j)
+            nrm = normed(at, j)
+            f = sigmoid(forget[at, cols] + mix_f[0:1, cols] * nrm + bias_f[0:1, cols])
+            o = sigmoid(gate[at, cols] + mix_r[0:1, cols] * nrm + bias_r[0:1, cols])
+            forget[at, cols] = f
+            gate[at, cols] = o
+            inject = (1.0 - f) * cand[at, cols]
+            keep = f * mask
+            for t in range(BLOCK):
+                now = slice(t * rows, (t + 1) * rows)
+                a_list[j] = a_list[j] * keep[now]
+                b_list[j] = b_list[j] * keep[now] + inject[now]
+        return tuple(a_list), tuple(b_list)
+
+    def gather_step(ch, runs, h0=0, h1=blocks):
+        entire = h1 - h0 == blocks
+        if entire:
+            pl.when(ch + 2 < chunks - 1)(lambda: send_tokens(ch + 2, 0, blocks))
+            pl.when(ch + 2 == chunks - 1)(send_last)
             cot_copy(ch + 1).start()
 
         base = pl.multiple_of(ch * span, span)
         slot = lax.rem(ch, 2)
 
-        x_copy(ch).wait_recv()
-        d_copy(ch).start()
-        cot_copy(ch).wait()
-        for h in range(blocks):
-            for j in range(tiles):
-                v = cot_raw[slot, :, h * BLOCK : (h + 1) * BLOCK, lanes(j)].astype(F32).reshape(part, LANE)
-                cot[pl.ds(pl.multiple_of(base + h * part, part), part), lanes(j)] = swapped(v, rows, BLOCK).astype(BF16)
-        pl.when(ch >= 1)(lambda: flip(ch - 1))
-        own_copy(ch).wait()
-        s_copy(ch).wait_recv()
-        d_copy(ch).wait_recv()
+        arrived(ch, across, h0, h1, x_move).wait_recv()
+        d_copy(ch, h0, h1).start()
+
+        if h0 == 0:
+            runs = lax.fori_loop(jnp.maximum(ch - 1, 0) * blocks, ch * blocks, gates, runs)
+        else:
+            runs = lax.fori_loop(ch * blocks, ch * blocks + h0, gates, runs)
+
+        if h0 == 0:
+            cot_copy(ch).wait()
+            for h in range(blocks):
+                for j in range(tiles):
+                    v = cot_raw[slot, :, h * BLOCK : (h + 1) * BLOCK, lanes(j)].astype(F32).reshape(part, LANE)
+                    at = pl.ds(pl.multiple_of(base + h * part, part), part)
+                    cot[at, lanes(j)] = swapped(v, rows, BLOCK).astype(BF16)
+            pl.when(ch >= 2)(lambda: keep_copy(ch - 2).wait())
+        arrived(ch, chan, h0, h1, own_move).wait()
+        arrived(ch, sibling, h0, h1, s_move).wait_recv()
+        d_copy(ch, h0, h1).wait_recv()
 
         first = pl.multiple_of(ch * chan_count * span, span)
 
-        def tokens_at(block, r, t0, cols):
-            at = pl.multiple_of(first + block * span + r * CHUNK + t0, BLOCK)
+        def tokens_at(block, r, h, cols):
+            at = pl.multiple_of(first + block * span + h * part + r * BLOCK, BLOCK)
             return raw[pl.ds(at, BLOCK), cols].astype(F32)
 
         def each(i, turn):
-            r, h = i // blocks, lax.rem(i, blocks)
+            r, h = lax.rem(i, rows), h0 + i // rows
             totals = [jnp.zeros((BLOCK, LANE), F32) for _ in range(chan_count)]
             for j in range(tiles):
                 for b in range(chan_count):
-                    totals[b] = totals[b] + turn(tokens_at(b, r, h * BLOCK, lanes(j)))
+                    totals[b] = totals[b] + turn(tokens_at(b, r, h, lanes(j)))
             while len(totals) > 1:
                 totals = [a + b for a, b in zip(totals[::2], totals[1::2])]
             part_s[h, r] = totals[0]
@@ -217,27 +244,29 @@
             each(i, lambda v: v)
             return carry
 
-        lax.fori_loop(0, rows * blocks, sum_rows, 0, unroll=2)
-        mean_s[...] = jnp.broadcast_to(jnp.sum(part_s[...], axis=-1, keepdims=True) * (1.0 / full), mean_s.shape)
+        count = (h1 - h0) * rows
+        stat = (h1 - h0,) + mean_s.shape[1:]
+        lax.fori_loop(0, count, sum_rows, 0, unroll=2)
+        total = jnp.sum(part_s[h0:h1], axis=-1, keepdims=True)
+        mean_s[h0:h1] = jnp.broadcast_to(total * (1.0 / full), stat)
 
         def square_rows(i, carry):
-            r, h = i // blocks, lax.rem(i, blocks)
-            m = mean_s[h, r]
+            m = mean_s[h0 + i // rows, lax.rem(i, rows)]
             each(i, lambda v: (v - m) * (v - m))
             return carry
 
-        lax.fori_loop(0, rows * blocks, square_rows, 0, unroll=2)
-        var = jnp.sum(part_s[...], axis=-1, keepdims=True) * (1.0 / full)
-        inv_s[...] = jnp.broadcast_to(lax.rsqrt(var + EPSILON), inv_s.shape)
-
-        for h in range(blocks):
+        lax.fori_loop(0, count, square_rows, 0, unroll=2)
+        var = jnp.sum(part_s[h0:h1], axis=-1, keepdims=True) * (1.0 / full)
+        inv_s[h0:h1] = jnp.broadcast_to(lax.rsqrt(var + EPSILON), stat)
+
+        for h in range(h0, h1):
             mean_h = mean_s[h].reshape(part, LANE)
             inv_h = inv_s[h].reshape(part, LANE)
 
             def normalize(j, carry, h=h, mean_h=mean_h, inv_h=inv_h):
                 cols = pl.ds(pl.multiple_of(j * LANE, LANE), LANE)
                 inner = pl.ds(pl.multiple_of(lax.rem(j, tiles) * LANE, LANE), LANE)
-                v = jnp.concatenate([tokens_at(j // tiles, r, h * BLOCK, inner) for r in range(rows)], axis=0)
+                v = jnp.concatenate([tokens_at(j // tiles, r, h, inner) for r in range(rows)], axis=0)
                 v = (v - mean_h) * inv_h * gain[0:1, cols] + shift[0:1, cols]
                 low[slot, h * part : (h + 1) * part, cols] = swapped(v, rows, BLOCK).astype(BF16)
                 return carry
@@ -247,44 +276,31 @@
             mean[at, :] = swapped(mean_h, rows, BLOCK)
             inv[at, :] = swapped(inv_h, rows, BLOCK)
             for j in range(tiles):
-                v = jnp.concatenate([tokens_at(chan, r, h * BLOCK, lanes(j)) for r in range(rows)], axis=0)
+                v = jnp.concatenate([tokens_at(chan, r, h, lanes(j)) for r in range(rows)], axis=0)
                 own_tok[at, lanes(j)] = swapped(v, rows, BLOCK).astype(BF16)
 
-        at = pl.ds(base, span)
-
-        @pl.when(ch == 0)
-        def _():
-            for copy in w_copies:
-                copy.wait()
-
-        cand[at, :] = jnp.dot(low[slot], w_buf[0], preferred_element_type=F32)
-        forget[at, :] = jnp.dot(low[slot], w_buf[1], preferred_element_type=F32)
-        gate[at, :] = jnp.dot(low[slot], w_buf[2], preferred_element_type=F32)
-
-        def gates(b, carry):
-            a_list, b_list = list(carry[0]), list(carry[1])
-            at = pl.ds(pl.multiple_of(base + b * part, part), part)
-            mask = keep_mask[at, :]
-            for j in range(tiles):
-                cols = lanes(j)
-                nrm = normed(at, j)
-                f = sigmoid(forget[at, cols] + mix_f[0:1, cols] * nrm + bias_f[0:1, cols])
-                o = sigmoid(gate[at, cols] + mix_r[0:1, cols] * nrm + bias_r[0:1, cols])
-                forget[at, cols] = f
-                gate[at, cols] = o
-                inject = (1.0 - f) * cand[at, cols]
-                keep = f * mask
-                for t in range(BLOCK):
-                    now = slice(t * rows, (t + 1) * rows)
-                    a_list[j] = a_list[j] * keep[now]
-                    b_list[j] = b_list[j] * keep[now] + inject[now]
-            return tuple(a_list), tuple(b_list)
-
-        return lax.fori_loop(0, blocks, gates, (a_run, b_run))
+        if entire:
+
+            @pl.when(ch == 0)
+            def _():
+                for copy in w_copies:
+                    copy.wait()
+
+        at = pl.ds(pl.multiple_of(base + h0 * part, part), (h1 - h0) * part)
+        for k, ref in enumerate((cand, forget, gate)):
+            ref[at, :] = jnp.dot(low[slot, h0 * part : h1 * part], w_buf[k], preferred_element_type=F32)
+
+        if h1 == blocks:
+            keep_copy(ch).start()
+
+        return runs
 
     ones = tuple(jnp.ones((rows, LANE), F32) for _ in range(tiles))
     zeros = tuple(jnp.zeros((rows, LANE), F32) for _ in range(tiles))
-    a_run, b_run = lax.fori_loop(0, chunks, gather_step, (ones, zeros))
+    runs = lax.fori_loop(0, chunks - 1, gather_step, (ones, zeros))
+    for h in range(blocks):
+        runs = gather_step(chunks - 1, runs, h, h + 1)
+    a_run, b_run = lax.fori_loop(chunks * blocks - 1, chunks * blocks, gates, runs)
 
     spans = jnp.where(reset_rows[0] >= tm_count * steps, 1.0, 0.0)
     last_tm = tm_count - 1
@@ -320,7 +336,6 @@
     pl.when(tm < last_tm)(lambda: near_copy(0, tm + 1).start())
     peers(lambda p: far_copy(0, tm, p).start())
     pl.when(tm == last_tm)(lambda: peers(lambda p: last_copy(p).start()))
-    flip(chunks - 1)
     peers(lambda p: far_copy(0, p, tm).wait_recv())
     pl.when(tm > 0)(lambda: near_copy(0, tm).wait_recv())
 
@@ -336,7 +351,8 @@
         row = jnp.broadcast_to(here[j : j + 1], (rows, LANE))
         others = jnp.where(tm == 0, entry[:, lanes(j)], near[0, 1, :, lanes(j)])
         states.append(jnp.where(spans > 0, row, others))
-    tr_copy(chunks - 1).wait()
+    keep_copy(chunks - 2).wait()
+    keep_copy(chunks - 1).wait()
     low_copy(0).start()
 
     def forward(b, states):
@@ -367,8 +383,7 @@
 
     def start_later():
         flow[0] = jnp.ones((rows, width), F32)
-        for i in range(1, 4):
-            flow[i] = jnp.zeros((rows, width), F32)
+        flow[1] = jnp.zeros((rows, width), F32)
 
     def later(b, carry):
         ch, h = b // blocks, lax.rem(b, blocks)
@@ -391,7 +406,6 @@
             rest = 1.0 - o
             out = swapped(o * th + rest * x, BLOCK, rows).astype(BF16)
             act_buf[slot, :, pl.ds(t0, BLOCK), cols] = out.reshape(rows, BLOCK, LANE)
-            reset_pre = ct * (th - x) * o * rest
             direct = ct * o * (1.0 - th * th)
             side[at, cols] = (ct * rest).astype(BF16)
             gate[at, cols] = direct
@@ -402,8 +416,6 @@
                 run = run * keep[now]
                 total = total + run * direct[now]
             flow[0, :, cols], flow[1, :, cols] = run, total
-            for i, v in enumerate((reset_pre * normed(at, j), reset_pre)):
-                flow[2 + i, :, cols] = flow[2 + i, :, cols] + jnp.sum(v.reshape(BLOCK, rows, LANE), axis=0)
 
         @pl.when(h == blocks - 1)
         def _():
@@ -419,16 +431,15 @@
         peers(lambda p: far_copy(1, tm, p).start())
         for target in (sibling, across):
             pl.semaphore_signal(ready_sem, inc=1, device_id=(tm, target), device_id_type=MESH)
-        for i in range(2):
-            sum_rx[tm, 2 * i + 1 : 2 * i + 2, :] = jnp.sum(flow[2 + i], axis=0, keepdims=True)
-        sum_rx[tm, 6:8, :] = jnp.zeros((2, width), F32)
         more[...] = jnp.zeros_like(more)
 
     def sent_on(ch, carry):
-        d_copy(ch).wait_send()
+        d_copy(ch, 0, blocks).wait_send()
         return carry
 
-    lax.fori_loop(0, chunks, sent_on, 0)
+    lax.fori_loop(0, chunks - 1, sent_on, 0)
+    for h in range(blocks):
+        d_copy(chunks - 1, h, h + 1).wait_send()
 
     n = tm_count // 2
     o, y = tm // 2, lax.rem(tm, 2)
@@ -620,11 +631,13 @@
         pick = lax.broadcasted_iota(jnp.int32, (8, LANE), 0)
         for j in range(tiles):
             cols = lanes(j)
-            own = grad_buf[1, at, cols].astype(F32) * mix_f[0:1, cols] + grad_buf[2, at, cols].astype(F32) * mix_r[0:1, cols]
-            g = cand[at, cols] + cot[at, cols].astype(F32) + own
+            fp, rp = grad_buf[1, at, cols].astype(F32), grad_buf[2, at, cols].astype(F32)
+            g = cand[at, cols] + cot[at, cols].astype(F32) + fp * mix_f[0:1, cols] + rp * mix_r[0:1, cols]
             cand[at, cols] = g
-            weighted = g * hat(at, j)
-            for i, v in enumerate((weighted, g)):
+            h = hat(at, j)
+            nrm = h * mine(gain, j) + mine(shift, j)
+            weighted = g * h
+            for i, v in enumerate((fp * nrm, rp * nrm, fp, rp, weighted, g)):
                 more[i, :, cols] = more[i, :, cols] + jnp.sum(v.reshape(CHUNK, rows, LANE), axis=0)
             for i, v in enumerate((g * mine(gain, j), weighted * mine(gain, j))):
                 lead = jnp.where(pick == i, 1.0, 0.0).astype(BF16)
@@ -658,9 +671,9 @@
         out_copy(ch).start()
 
     def share_sums():
-        for i in range(2):
-            sum_rx[tm, 2 * i : 2 * i + 1, :] = jnp.sum(flow[1 + i], axis=0, keepdims=True)
-            sum_rx[tm, 4 + i : 5 + i, :] = jnp.sum(more[i], axis=0, keepdims=True)
+        for i in range(6):
+            sum_rx[tm, i : i + 1, :] = jnp.sum(more[i], axis=0, keepdims=True)
+        sum_rx[tm, 6:8, :] = jnp.zeros((2, width), F32)
         peers(lambda p: sum_copy(tm, p).start())
 
     def start_backward():
@@ -676,8 +689,6 @@
             row = jnp.broadcast_to(inflow[j : j + 1], (rows, LANE))
             others = jnp.where(tm == last_tm, 0.0, near[1, 1, :, lanes(j)])
             flow[0, :, lanes(j)] = jnp.where(spans > 0, row, others)
-        flow[1] = jnp.zeros((rows, width), F32)
-        flow[2] = jnp.zeros((rows, width), F32)
 
     def backward(i, carry):
         b = steps // BLOCK - 1 - i
@@ -699,9 +710,40 @@
             forget_pre = cand_grad * (masked[at, cols] - cand[at, cols]) * f
             grad_buf[0, at, cols] = cand_grad.astype(BF16)
             grad_buf[1, at, cols] = forget_pre.astype(BF16)
-            for i, v in enumerate((forget_pre * normed(at, j), forget_pre)):
-                flow[1 + i, :, cols] = flow[1 + i, :, cols] + jnp.sum(v.reshape(BLOCK, rows, LANE), axis=0)
         return carry
+
+    def close_tokens(ch, carry, h0=0, h1=blocks):
+        arrived(ch, chan, h0, h1, x_move).wait_send()
+        arrived(ch, chan, h0, h1, s_move).wait_send()
+        return carry
+
+    def close_first():
+        lax.fori_loop(0, chunks - 1, close_tokens, 0)
+        for h in range(blocks):
+            close_tokens(chunks - 1, 0, h, h + 1)
+        for way in range(2):
+            peers(lambda p, way=way: far_copy(way, tm, p).wait_send())
+        pl.when(tm < last_tm)(lambda: near_copy(0, tm).wait_send())
+        pl.when(tm > 0)(lambda: near_copy(1, tm).wait_send())
+        pl.when(tm == last_tm)(lambda: peers(lambda p: last_copy(p).wait_send()))
+        pl.when(tm != last_tm)(lambda: last_copy(tm).wait_recv())
+        for ch in (chunks - 2, chunks - 1):
+            act_copy(ch).wait()
+        for j in range(tiles):
+            row = jnp.broadcast_to(last[j : j + 1], (rows, LANE))
+            others = jnp.where(tm == last_tm, near[0, 0, :, lanes(j)], near[0, 2, :, lanes(j)])
+            final[:, lanes(j)] = jnp.where(spans > 0, row, others)
+
+    def close_second():
+        for ch in range(chunks - 4, chunks):
+            for d in range(1, 4):
+                row_copy(ch, chan, d).wait_send()
+        for ch in (chunks - 2, chunks - 1):
+            out_copy(ch).wait()
+            acr_copy(ch).wait_send()
+        peers(lambda p: sum_copy(p, tm).wait_recv())
+        peers(lambda p: sum_copy(tm, p).wait_send())
+        totals[...] = lax.fori_loop(0, tm_count, lambda d, v: v + sum_rx[d], jnp.zeros(totals.shape, F32))
 
     def slot_step(s, carry):
         u, go = stage(s, give_stage)
@@ -751,7 +793,9 @@
         def _():
             pl.when(u0 + 1 < units)(lambda: low_copy(u0 + 1).start())
             low_copy(u0).wait()
-            g = jnp.dot(low[lax.rem(u0, 2)], grad_buf[gate_of(u0)], preferred_element_type=F32)
+            g = lax.dot_general(
+                left_buf[lax.rem(u0, 2)], grad_buf[gate_of(u0)], (((0,), (0,)), ((), ())), preferred_element_type=F32
+            )
             raw[pl.ds(pl.multiple_of(u0 * UNIT, UNIT), UNIT)] = g.astype(BF16)
             launch(pair_copy, u0)
             for l, c, reach, first, parity in lines[1:]:
@@ -802,10 +846,12 @@
         for job, offset in ((finish, 5), (full_sum, 3), (chip_sum, 1), (project, 0)):
             at = s - FIRST - offset
             pl.when(both(at >= 0, lax.rem(at, 2) == 0, at // 2 < chunks))(lambda job=job, at=at: job(at // 2))
+        pl.when(s == FIRST + 3)(close_first)
         pl.when(s == FIRST + 2 * chunks + 2)(share_sums)
+        pl.when(s == FIRST + 2 * chunks + 6)(close_second)
         return carry
 
-    slots = max((units - 1) * space + depth + 1, FIRST + 2 * chunks + 4)
+    slots = max((units - 1) * space + depth + 1, FIRST + 2 * chunks + 7)
     lax.fori_loop(0, slots, slot_step, 0)
 
     def close_unit(u, carry):
@@ -825,36 +871,6 @@
 
     lax.fori_loop(units - SENDS, units, close_unit, 0)
 
-    def close_chunk(ch, carry):
-        x_copy(ch).wait_send()
-        s_copy(ch).wait_send()
-
-        @pl.when(ch >= chunks - 4)
-        def _():
-            for d in range(1, 4):
-                row_copy(ch, chan, d).wait_send()
-
-        return carry
-
-    lax.fori_loop(0, chunks, close_chunk, 0)
-    for ch in (chunks - 2, chunks - 1):
-        out_copy(ch).wait()
-        act_copy(ch).wait()
-        acr_copy(ch).wait_send()
-    for way in range(2):
-        peers(lambda p, way=way: far_copy(way, tm, p).wait_send())
-    pl.when(tm < last_tm)(lambda: near_copy(0, tm).wait_send())
-    pl.when(tm > 0)(lambda: near_copy(1, tm).wait_send())
-    pl.when(tm == last_tm)(lambda: peers(lambda p: last_copy(p).wait_send()))
-    pl.when(tm != last_tm)(lambda: last_copy(tm).wait_recv())
-    for j in range(tiles):
-        row = jnp.broadcast_to(last[j : j + 1], (rows, LANE))
-        others = jnp.where(tm == last_tm, near[0, 0, :, lanes(j)], near[0, 2, :, lanes(j)])
-        final[:, lanes(j)] = jnp.where(spans > 0, row, others)
-    peers(lambda p: sum_copy(p, tm).wait_recv())
-    peers(lambda p: sum_copy(tm, p).wait_send())
-    totals[...] = lax.fori_loop(0, tm_count, lambda d, v: v + sum_rx[d], jnp.zeros(totals.shape, F32))
-
 
 def layer(tokens, weights, cotangent, gain, shift, mix_f, mix_r, bias_f, bias_r, bank, selector, resets):
     rows, steps, width = tokens.shape
@@ -862,6 +878,7 @@
     tm_count, chan_count = lax.axis_size("tm"), lax.axis_size("chan")
     chunks = steps // CHUNK
     span = CHUNK * rows
+    pieces = chunks - 1 + CHUNK // BLOCK
     count = steps * rows
     units = 3 * full // UNIT
     ring = ring_of(tm_count)
@@ -879,7 +896,7 @@
             jax.ShapeDtypeStruct((units * UNIT, width), BF16),
             jax.ShapeDtypeStruct(tokens.shape, F32),
             jax.ShapeDtypeStruct(tokens.shape, BF16),
-            jax.ShapeDtypeStruct((full, count), BF16),
+            jax.ShapeDtypeStruct((count, full), BF16),
             jax.ShapeDtypeStruct((rows, width), F32),
             jax.ShapeDtypeStruct((8, width), F32),
         ),
@@ -889,7 +906,7 @@
             pltpu.VMEM((chunks * chan_count * span, width), BF16),
             pltpu.VMEM((ring * (3 * PAIR + 4 * LINE), width), BF16),
             pltpu.VMEM((2, span, full), BF16),
-            pltpu.VMEM((full, span), BF16),
+            pltpu.VMEM((2, count, UNIT), BF16),
             pltpu.VMEM((3, full, width), BF16),
             wide, wide, wide, wide,
             short,
@@ -902,16 +919,16 @@
             pltpu.VMEM((2, chan_count, span, width), BF16),
             pltpu.VMEM((2, rows, CHUNK, width), F32),
             pltpu.VMEM((chunks, 4, 8, span), F32),
-            pltpu.VMEM((2, rows, width), F32),
+            pltpu.VMEM((6, rows, width), F32),
             pltpu.VMEM((tm_count, 8, width), F32),
             stat, stat, stat,
             pltpu.VMEM((rows, width), F32),
             pltpu.VMEM((2, 3, rows, width), F32),
             pltpu.VMEM((2, tm_count, 8, LANE), F32),
-            pltpu.VMEM((4, rows, width), F32),
+            pltpu.VMEM((2, rows, width), F32),
             pltpu.VMEM((resets.shape[1], rows, LANE), jnp.int32),
-            dma((chunks,)), dma((chunks,)), dma((chunks,)), dma((chunks,)), dma((chunks,)), dma((chunks,)), dma((chunks,)),
-            dma((3,)), dma((2,)), dma((2,)), dma(()), dma((2,)),
+            dma((pieces,)), dma((pieces,)), dma((pieces,)), dma((pieces,)), dma((pieces,)), dma((pieces,)), dma((pieces,)),
+            dma((3,)), dma((2,)), dma((2,)), dma((2,)), dma((2,)),
             dma((2,)), dma((2,)), dma((2, tm_count)), dma((2, tm_count)), dma((tm_count,)), dma(()),
             pltpu.SemaphoreType.REGULAR,
             dma((2,)), dma((3, SENDS)), dma((SENDS,)), dma((3, SENDS)), dma((3, SENDS, 2)), dma((3, ring)), dma((SENDS,)),

time: 210 us -> 206 us (0.981)
  Pallas kernels: 209 us -> 205 us
    pallas_call x1, Pallas kernels: 197 us -> 193 us  [layer(): pl.pallas_call(layer_kernel, out_shape=(jax.ShapeDtypeStruct((units * UNI...]
where the time goes in v4:
time: 206 us; the launch traced here: 205 us
  Pallas kernels  205 us (100%)
    pallas_call x1, Pallas kernels, layer(): pl.pallas_call(layer_kernel, out_shape=(jax.ShapeDtypeStruct((units * UNI...  193 us
    pallas_call x1, Pallas kernels, tail(): pl.pallas_call(tail_kernel, out_shape=(jax.ShapeDtypeStruct(flat.shape, F...  11.8 us

profile of v4, /device:TPU:0, one launch (start us, length us, event | category | flops | bytes accessed | tf_op | source)
XLA Modules:
  0.0 205.3 jit_solution(18109029838820686931)
XLA Ops:
  0.6 192.9 %whole.1 = (bf16[6144,512]{1,0:T(8,128)(2,1)}, f32[8,256,512]{2,1,0:T(8,128)}, bf16[8,256,512]{2,1,0:T(8,128)(2,1)}, bf16[2048,2048]{1,0:T(8,128)(2,1)}, f32[8,512]{1,0:T(8,128)}, /*index=5*/f32[8,512]{1,0:T(8,128)}) custom-call(bf16[8,256,512]{2,1,0:T(8,128)(2,1)} %tokens.1, bf16[3,2048,512]{2,1,0:T(8,128)(2,1)} %weights.1, bf16[8,256,512]{2,1,0:T(8,128)(2,1)} %cotangent.1, ...), custom_call_target="tpu_custom_call" | custom-call | tf_op jit(solution)/shard_map/whole/pallas_call | solution.py:893
  193.5 11.8 %tail.1 = (f32[6144,512]{1,0:T(8,128)}, f32[8,256,512]{2,1,0:T(8,128)}, bf16[8,256,512]{2,1,0:T(8,128)(2,1)}, f32[8,512]{1,0:T(8,128)}, f32[1,512]{1,0:T(1,128)}...) custom-call(bf16[6144,512]{1,0:T(8,128)(2,1)} %get-tuple-element.25.fin, ...), custom_call_target="tpu_custom_call" | custom-call | tf_op jit(solution)/shard_map/tail/pallas_call | solution.py:996

commit v5 on v4

--- a/solution.py
+++ b/solution.py
@@ -13,11 +13,12 @@
 LAG = 2
 PAIR = 80
 LINE = 48
-SENDS = 4
+SENDS = 2
 VMEM_BYTES = 63 << 20
 TAIL = 4
 LATER = 4
-FIRST = 8
+OUTPUT = 8
+FIRST = 12
 MESH = pl.DeviceIdType.MESH
 F32 = jnp.float32
 BF16 = jnp.bfloat16
@@ -44,10 +45,10 @@
 
 def layer_kernel(
     tokens, weights, cotangent, gain, shift, mix_f, mix_r, bias_f, bias_r, bank, selector, resets,
-    fin, in_grad, act, low_all, final, totals,
-    raw, rx, low, left_buf, w_buf, cand, forget, gate, masked, own_tok, cot_raw, cot, mean, inv, keep_mask, grad_buf,
+    fin, in_grad, act, low_t, final, totals,
+    raw, rx, low, low_t_buf, w_buf, cand, forget, gate, masked, own_tok, cot_raw, cot, mean, inv, keep_mask, grad_buf,
     act_buf, side, terms, out_buf, row_rx, more, sum_rx, mean_s, inv_s, part_s, entry, near, far, flow, reset_rows,
-    x_send, x_recv, s_send, s_recv, d_send, d_recv, own_sem, w_sem, cot_sem, act_sem, keep_sem, low_sem,
+    x_send, x_recv, s_send, s_recv, d_send, d_recv, own_sem, w_sem, cot_sem, act_sem, tr_sem, low_sem,
     near_send, near_recv, far_send, far_recv, last_send, last_recv, ready_sem, out_sem, loc_sem, pair_send, red_send,
     bc_send, bc_recv, swap_send, give_send, give_recv, rx_recv, sib_send, sib_recv, acr_send, acr_recv, row_send,
     row_recv, sum_send, sum_recv,
@@ -95,26 +96,23 @@
         ]
 
     def own_move(src, dst, sem):
-        return pltpu.make_async_copy(src, dst, own_sem.at[sem])
+        return pltpu.make_async_copy(src, dst, own_sem)
 
     def x_move(src, dst, sem):
-        return remote(src, dst, x_send.at[sem], x_recv.at[sem], (tm, across))
+        return remote(src, dst, x_send, x_recv.at[sem], (tm, across))
 
     def s_move(src, dst, sem):
-        return remote(src, dst, s_send.at[sem], s_recv.at[sem], (tm, sibling))
+        return remote(src, dst, s_send, s_recv, (tm, sibling))
 
     def arrived(ch, block, h0, h1, copy):
         here = raw.at[raw_rows(ch, block, h0, h1)]
         return copy(here, here, ch + h0)
 
-    def send_tokens(ch, h0, h1):
-        for copy in (own_move, x_move, s_move):
-            for c in token_copies(ch, h0, h1, copy):
-                c.start()
-
     def d_copy(ch, h0, h1):
         view = raw.at[raw_rows(ch, across, h0, h1)]
-        return remote(view, view, d_send.at[ch + h0], d_recv.at[ch + h0], (tm, sibling))
+        return remote(view, view, d_send, d_recv.at[ch + h0], (tm, sibling))
+
+    all_tokens = raw.at[pl.ds(0, steps * rows)]
 
     def cot_copy(ch):
         at = pl.ds(pl.multiple_of(ch * CHUNK, CHUNK), CHUNK)
@@ -124,12 +122,12 @@
         at = pl.ds(pl.multiple_of(ch * CHUNK, CHUNK), CHUNK)
         return pltpu.make_async_copy(act_buf.at[lax.rem(ch, 2)], act.at[:, at, :], act_sem.at[lax.rem(ch, 2)])
 
-    def keep_copy(ch):
-        return pltpu.make_async_copy(low.at[lax.rem(ch, 2)], low_all.at[rows_of(ch)], keep_sem.at[lax.rem(ch, 2)])
+    def tr_copy(ch):
+        return pltpu.make_async_copy(low_t_buf, low_t.at[:, rows_of(ch)], tr_sem)
 
     def low_copy(u):
         at = pl.ds(pl.multiple_of(lax.rem(u, per_gate) * UNIT, UNIT), UNIT)
-        return pltpu.make_async_copy(low_all.at[:, at], left_buf.at[lax.rem(u, 2)], low_sem.at[lax.rem(u, 2)])
+        return pltpu.make_async_copy(low_t.at[at], low.at[lax.rem(u, 2)], low_sem.at[lax.rem(u, 2)])
 
     w_copies = [pltpu.make_async_copy(weights.at[k], w_buf.at[k], w_sem.at[k]) for k in range(3)]
 
@@ -142,16 +140,25 @@
         return carry
 
     lax.fori_loop(1, tm_count, greet, 0)
-    for ch in range(2):
+    def start_own(ch, carry):
         for copy in token_copies(ch, 0, blocks, own_move):
             copy.start()
+        return carry
+
+    def start_sibling(ch, carry):
+        for copy in token_copies(ch, 0, blocks, s_move):
+            copy.start()
+        return carry
+
+    lax.fori_loop(0, chunks, start_own, 0)
     cot_copy(0).start()
     for copy in w_copies:
         copy.start()
     pl.semaphore_wait(barrier, tm_count + 2)
     for ch in range(2):
-        for copy in token_copies(ch, 0, blocks, x_move) + token_copies(ch, 0, blocks, s_move):
+        for copy in token_copies(ch, 0, blocks, x_move):
             copy.start()
+    lax.fori_loop(0, chunks, start_sibling, 0)
 
     count = resets.shape[1]
     for j in range(count):
@@ -171,9 +178,32 @@
     for r in range(rows):
         entry[r : r + 1, :] = bank[pl.ds(selector[r], 1), :]
 
+    def flip(ch):
+        @pl.when(ch >= 1)
+        def _():
+            tr_copy(ch - 1).wait()
+
+        def one(j, carry):
+            cols = pl.ds(pl.multiple_of(j * 256, 256), 256)
+            low_t_buf[cols, :] = jnp.transpose(low[lax.rem(ch, 2), :, cols])
+            return carry
+
+        lax.fori_loop(0, full // 256, one, 0, unroll=2)
+        tr_copy(ch).start()
+
+    def project_one(ch, k, h0, h1):
+        at = pl.ds(pl.multiple_of(ch * span + h0 * part, part), (h1 - h0) * part)
+        ref = (cand, forget, gate)[k]
+        ref[at, :] = jnp.dot(low[lax.rem(ch, 2), h0 * part : h1 * part], w_buf[k], preferred_element_type=F32)
+
+    def send_across(ch):
+        for copy in token_copies(ch, 0, blocks, x_move):
+            copy.start()
+
     def send_last():
         for h in range(blocks):
-            send_tokens(chunks - 1, h, h + 1)
+            for copy in token_copies(chunks - 1, h, h + 1, x_move):
+                copy.start()
 
     def gates(b, carry):
         a_list, b_list = list(carry[0]), list(carry[1])
@@ -197,7 +227,7 @@
     def gather_step(ch, runs, h0=0, h1=blocks):
         entire = h1 - h0 == blocks
         if entire:
-            pl.when(ch + 2 < chunks - 1)(lambda: send_tokens(ch + 2, 0, blocks))
+            pl.when(ch + 2 < chunks - 1)(lambda: send_across(ch + 2))
             pl.when(ch + 2 == chunks - 1)(send_last)
             cot_copy(ch + 1).start()
 
@@ -207,6 +237,12 @@
         arrived(ch, across, h0, h1, x_move).wait_recv()
         d_copy(ch, h0, h1).start()
 
+        if entire:
+            pl.when(ch >= 1)(lambda: project_one(ch - 1, 2, 0, blocks))
+        elif h0 == 0:
+            project_one(ch - 1, 2, 0, blocks)
+        else:
+            project_one(ch, 2, 0, h0)
         if h0 == 0:
             runs = lax.fori_loop(jnp.maximum(ch - 1, 0) * blocks, ch * blocks, gates, runs)
         else:
@@ -219,9 +255,15 @@
                     v = cot_raw[slot, :, h * BLOCK : (h + 1) * BLOCK, lanes(j)].astype(F32).reshape(part, LANE)
                     at = pl.ds(pl.multiple_of(base + h * part, part), part)
                     cot[at, lanes(j)] = swapped(v, rows, BLOCK).astype(BF16)
-            pl.when(ch >= 2)(lambda: keep_copy(ch - 2).wait())
-        arrived(ch, chan, h0, h1, own_move).wait()
-        arrived(ch, sibling, h0, h1, s_move).wait_recv()
+        if entire:
+
+            @pl.when(ch == 0)
+            def _():
+                own_move(all_tokens, all_tokens, 0).wait()
+                s_move(all_tokens, all_tokens, 0).wait_recv()
+                for copy in w_copies:
+                    copy.wait()
+
         d_copy(ch, h0, h1).wait_recv()
 
         first = pl.multiple_of(ch * chan_count * span, span)
@@ -279,20 +321,10 @@
                 v = jnp.concatenate([tokens_at(chan, r, h, lanes(j)) for r in range(rows)], axis=0)
                 own_tok[at, lanes(j)] = swapped(v, rows, BLOCK).astype(BF16)
 
+        project_one(ch, 0, h0, h1)
+        project_one(ch, 1, h0, h1)
         if entire:
-
-            @pl.when(ch == 0)
-            def _():
-                for copy in w_copies:
-                    copy.wait()
-
-        at = pl.ds(pl.multiple_of(base + h0 * part, part), (h1 - h0) * part)
-        for k, ref in enumerate((cand, forget, gate)):
-            ref[at, :] = jnp.dot(low[slot, h0 * part : h1 * part], w_buf[k], preferred_element_type=F32)
-
-        if h1 == blocks:
-            keep_copy(ch).start()
-
+            flip(ch)
         return runs
 
     ones = tuple(jnp.ones((rows, LANE), F32) for _ in range(tiles))
@@ -300,6 +332,7 @@
     runs = lax.fori_loop(0, chunks - 1, gather_step, (ones, zeros))
     for h in range(blocks):
         runs = gather_step(chunks - 1, runs, h, h + 1)
+    project_one(chunks - 1, 2, blocks - 1, blocks)
     a_run, b_run = lax.fori_loop(chunks * blocks - 1, chunks * blocks, gates, runs)
 
     spans = jnp.where(reset_rows[0] >= tm_count * steps, 1.0, 0.0)
@@ -313,14 +346,22 @@
 
     def far_copy(way, source, target):
         return remote(
-            far.at[way, source], far.at[way, source], far_send.at[way, target], far_recv.at[way, source], (target, chan)
+            far.at[way, source], far.at[way, source], far_send.at[way], far_recv.at[way], (target, chan)
         )
 
+    def far_all(way):
+        maps = far.at[way, pl.ds(0, tm_count - 1)]
+        return remote(maps, maps, far_send.at[way], far_recv.at[way], (tm, sibling))
+
     def last_copy(target):
-        return remote(near.at[0, 0], near.at[0, 2], last_send.at[target], last_recv, (target, chan))
+        return remote(near.at[0, 0], near.at[0, 2], last_send, last_recv, (target, chan))
+
+    def last_all():
+        sent = sum_rx.at[pl.ds(0, tm_count - 1)]
+        remote(sent, sent, last_send, last_recv, (tm, sibling)).wait_send()
 
     def sum_copy(source, target):
-        return remote(sum_rx.at[source], sum_rx.at[source], sum_send.at[target], sum_recv.at[source], (target, chan))
+        return remote(sum_rx.at[source], sum_rx.at[source], sum_send, sum_recv, (target, chan))
 
     def peers(act_on):
         def one(d, carry):
@@ -336,7 +377,8 @@
     pl.when(tm < last_tm)(lambda: near_copy(0, tm + 1).start())
     peers(lambda p: far_copy(0, tm, p).start())
     pl.when(tm == last_tm)(lambda: peers(lambda p: last_copy(p).start()))
-    peers(lambda p: far_copy(0, p, tm).wait_recv())
+    flip(chunks - 1)
+    far_all(0).wait_recv()
     pl.when(tm > 0)(lambda: near_copy(0, tm).wait_recv())
 
     def carry_on(d, carry):
@@ -351,8 +393,7 @@
         row = jnp.broadcast_to(here[j : j + 1], (rows, LANE))
         others = jnp.where(tm == 0, entry[:, lanes(j)], near[0, 1, :, lanes(j)])
         states.append(jnp.where(spans > 0, row, others))
-    keep_copy(chunks - 2).wait()
-    keep_copy(chunks - 1).wait()
+    tr_copy(chunks - 1).wait()
     low_copy(0).start()
 
     def forward(b, states):
@@ -386,28 +427,15 @@
         flow[1] = jnp.zeros((rows, width), F32)
 
     def later(b, carry):
-        ch, h = b // blocks, lax.rem(b, blocks)
-        slot = lax.rem(ch, 2)
-
-        @pl.when(both(h == 0, ch >= 2))
-        def _():
-            act_copy(ch - 2).wait()
-
         at = pl.ds(pl.multiple_of(b * part, part), part)
-        t0 = pl.multiple_of(h * BLOCK, BLOCK)
         mask = keep_mask[at, :]
         for j in range(tiles):
             cols = lanes(j)
             f = forget[at, cols]
             th = jnp.tanh(f * masked[at, cols] + (1.0 - f) * cand[at, cols])
             o = gate[at, cols]
-            x = own_tok[at, cols].astype(F32)
-            ct = cot[at, cols].astype(F32)
-            rest = 1.0 - o
-            out = swapped(o * th + rest * x, BLOCK, rows).astype(BF16)
-            act_buf[slot, :, pl.ds(t0, BLOCK), cols] = out.reshape(rows, BLOCK, LANE)
-            direct = ct * o * (1.0 - th * th)
-            side[at, cols] = (ct * rest).astype(BF16)
+            direct = cot[at, cols].astype(F32) * o * (1.0 - th * th)
+            side[at, cols] = o.astype(BF16)
             gate[at, cols] = direct
             keep = f * mask
             run, total = flow[0, :, cols], flow[1, :, cols]
@@ -416,12 +444,37 @@
                 run = run * keep[now]
                 total = total + run * direct[now]
             flow[0, :, cols], flow[1, :, cols] = run, total
+        return carry
+
+    def output(b, carry):
+        ch, h = b // blocks, lax.rem(b, blocks)
+        slot = lax.rem(ch, 2)
+
+        @pl.when(both(h == 0, ch >= 2))
+        def _():
+            act_copy(ch - 2).wait()
+
+        at = pl.ds(pl.multiple_of(b * part, part), part)
+        t0 = pl.multiple_of(h * BLOCK, BLOCK)
+        for j in range(tiles):
+            cols = lanes(j)
+            f = forget[at, cols]
+            th = jnp.tanh(f * masked[at, cols] + (1.0 - f) * cand[at, cols])
+            o = side[at, cols].astype(F32)
+            rest = 1.0 - o
+            out = swapped(o * th + rest * own_tok[at, cols].astype(F32), BLOCK, rows).astype(BF16)
+            act_buf[slot, :, pl.ds(t0, BLOCK), cols] = out.reshape(rows, BLOCK, LANE)
+            side[at, cols] = (cot[at, cols].astype(F32) * rest).astype(BF16)
 
         @pl.when(h == blocks - 1)
         def _():
             act_copy(ch).start()
 
         return carry
+
+    def end_output():
+        for target in (sibling, across):
+            pl.semaphore_signal(ready_sem, inc=1, device_id=(tm, target), device_id_type=MESH)
 
     def end_later():
         near[1, 0] = flow[1]
@@ -429,17 +482,9 @@
             far[1, tm, j : j + 1, :] = spanning(flow[1, :, lanes(j)])
         pl.when(tm > 0)(lambda: near_copy(1, tm - 1).start())
         peers(lambda p: far_copy(1, tm, p).start())
-        for target in (sibling, across):
-            pl.semaphore_signal(ready_sem, inc=1, device_id=(tm, target), device_id_type=MESH)
         more[...] = jnp.zeros_like(more)
 
-    def sent_on(ch, carry):
-        d_copy(ch, 0, blocks).wait_send()
-        return carry
-
-    lax.fori_loop(0, chunks - 1, sent_on, 0)
-    for h in range(blocks):
-        d_copy(chunks - 1, h, h + 1).wait_send()
+    remote(all_tokens, all_tokens, d_send, d_recv.at[0], (tm, sibling)).wait_send()
 
     n = tm_count // 2
     o, y = tm // 2, lax.rem(tm, 2)
@@ -581,9 +626,13 @@
 
     def row_copy(ch, source, d):
         return remote(
-            row_rx.at[ch, source], row_rx.at[ch, source], row_send.at[lax.rem(ch, 4), d - 1],
-            row_recv.at[lax.rem(ch, 4), source], (tm, lax.rem(chan + d, 4)),
+            row_rx.at[ch, source], row_rx.at[ch, source], row_send.at[lax.rem(ch, 4)], row_recv.at[lax.rem(ch, 4)],
+            (tm, lax.rem(chan + d, 4)),
         )
+
+    def row_all(ch):
+        sums = row_rx.at[ch, pl.ds(0, chan_count - 1)]
+        return remote(sums, sums, row_send.at[lax.rem(ch, 4)], row_recv.at[lax.rem(ch, 4)], (tm, sibling))
 
     def out_copy(ch):
         at = pl.ds(pl.multiple_of(ch * CHUNK, CHUNK), CHUNK)
@@ -646,13 +695,12 @@
                 for p in (high, low_part):
                     total = total + lax.dot_general(lead, p, (((1,), (1,)), ((), ())), preferred_element_type=F32)
         row_rx[ch, chan] = total
+        pl.when(ch >= 4)(lambda: row_all(ch - 4).wait_send())
         for d in range(1, 4):
-            pl.when(ch >= 4)(lambda d=d: row_copy(ch - 4, chan, d).wait_send())
             row_copy(ch, chan, d).start()
 
     def finish(ch):
-        for d in range(1, 4):
-            row_copy(ch, lax.rem(chan + d, 4), d).wait_recv()
+        row_all(ch).wait_recv()
 
         @pl.when(ch >= 2)
         def _():
@@ -667,7 +715,7 @@
             cols = lanes(j)
             g = cand[at, cols] * mine(gain, j)
             v = inv[at, :] * (g - first - hat(at, j) * second) + side[at, cols].astype(F32)
-            out_buf[lax.rem(ch, 2), :, :, cols] = swapped(v, CHUNK, rows).reshape(rows, CHUNK, LANE)
+            out_buf[lax.rem(ch, 2), :, :, cols] = swapped(v, CHUNK, rows).astype(BF16).reshape(rows, CHUNK, LANE)
         out_copy(ch).start()
 
     def share_sums():
@@ -677,7 +725,7 @@
         peers(lambda p: sum_copy(tm, p).start())
 
     def start_backward():
-        peers(lambda p: far_copy(1, p, tm).wait_recv())
+        far_all(1).wait_recv()
         pl.when(tm < last_tm)(lambda: near_copy(1, tm).wait_recv())
 
         def carry_back(i, v):
@@ -712,20 +760,14 @@
             grad_buf[1, at, cols] = forget_pre.astype(BF16)
         return carry
 
-    def close_tokens(ch, carry, h0=0, h1=blocks):
-        arrived(ch, chan, h0, h1, x_move).wait_send()
-        arrived(ch, chan, h0, h1, s_move).wait_send()
-        return carry
-
     def close_first():
-        lax.fori_loop(0, chunks - 1, close_tokens, 0)
-        for h in range(blocks):
-            close_tokens(chunks - 1, 0, h, h + 1)
+        x_move(all_tokens, all_tokens, 0).wait_send()
+        s_move(all_tokens, all_tokens, 0).wait_send()
         for way in range(2):
-            peers(lambda p, way=way: far_copy(way, tm, p).wait_send())
+            far_all(way).wait_send()
         pl.when(tm < last_tm)(lambda: near_copy(0, tm).wait_send())
         pl.when(tm > 0)(lambda: near_copy(1, tm).wait_send())
-        pl.when(tm == last_tm)(lambda: peers(lambda p: last_copy(p).wait_send()))
+        pl.when(tm == last_tm)(last_all)
         pl.when(tm != last_tm)(lambda: last_copy(tm).wait_recv())
         for ch in (chunks - 2, chunks - 1):
             act_copy(ch).wait()
@@ -736,13 +778,12 @@
 
     def close_second():
         for ch in range(chunks - 4, chunks):
-            for d in range(1, 4):
-                row_copy(ch, chan, d).wait_send()
+            row_all(ch).wait_send()
         for ch in (chunks - 2, chunks - 1):
             out_copy(ch).wait()
             acr_copy(ch).wait_send()
-        peers(lambda p: sum_copy(p, tm).wait_recv())
-        peers(lambda p: sum_copy(tm, p).wait_send())
+        sums = sum_rx.at[pl.ds(0, tm_count - 1)]
+        remote(sums, sums, sum_send, sum_recv, (tm, sibling)).wait()
         totals[...] = lax.fori_loop(0, tm_count, lambda d, v: v + sum_rx[d], jnp.zeros(totals.shape, F32))
 
     def slot_step(s, carry):
@@ -793,9 +834,7 @@
         def _():
             pl.when(u0 + 1 < units)(lambda: low_copy(u0 + 1).start())
             low_copy(u0).wait()
-            g = lax.dot_general(
-                left_buf[lax.rem(u0, 2)], grad_buf[gate_of(u0)], (((0,), (0,)), ((), ())), preferred_element_type=F32
-            )
+            g = jnp.dot(low[lax.rem(u0, 2)], grad_buf[gate_of(u0)], preferred_element_type=F32)
             raw[pl.ds(pl.multiple_of(u0 * UNIT, UNIT), UNIT)] = g.astype(BF16)
             launch(pair_copy, u0)
             for l, c, reach, first, parity in lines[1:]:
@@ -836,12 +875,21 @@
 
         pl.when(s == LATER - 1)(end_later)
         pl.when(s == LATER + 1)(start_backward)
-        share = -(-count // (FIRST - LATER - 1))
+        share = -(-count // (OUTPUT - LATER - 1))
         at2 = (s - LATER - 1) * share
 
-        @pl.when(both(s > LATER, s < FIRST))
+        @pl.when(both(s > LATER, s < OUTPUT))
         def _():
             lax.fori_loop(at2, jnp.minimum(at2 + share, count), backward, 0)
+
+        share = -(-count // (FIRST - OUTPUT))
+        at3 = (s - OUTPUT) * share
+
+        @pl.when(both(s >= OUTPUT, s < FIRST))
+        def _():
+            lax.fori_loop(at3, jnp.minimum(at3 + share, count), output, 0)
+
+        pl.when(s == FIRST - 1)(end_output)
 
         for job, offset in ((finish, 5), (full_sum, 3), (chip_sum, 1), (project, 0)):
             at = s - FIRST - offset
@@ -894,9 +942,9 @@
         layer_kernel,
         out_shape=(
             jax.ShapeDtypeStruct((units * UNIT, width), BF16),
-            jax.ShapeDtypeStruct(tokens.shape, F32),
             jax.ShapeDtypeStruct(tokens.shape, BF16),
-            jax.ShapeDtypeStruct((count, full), BF16),
+            jax.ShapeDtypeStruct(tokens.shape, BF16),
+            jax.ShapeDtypeStruct((full, count), BF16),
             jax.ShapeDtypeStruct((rows, width), F32),
             jax.ShapeDtypeStruct((8, width), F32),
         ),
@@ -906,7 +954,7 @@
             pltpu.VMEM((chunks * chan_count * span, width), BF16),
             pltpu.VMEM((ring * (3 * PAIR + 4 * LINE), width), BF16),
             pltpu.VMEM((2, span, full), BF16),
-            pltpu.VMEM((2, count, UNIT), BF16),
+            pltpu.VMEM((full, span), BF16),
             pltpu.VMEM((3, full, width), BF16),
             wide, wide, wide, wide,
             short,
@@ -917,7 +965,7 @@
             pltpu.VMEM((2, rows, CHUNK, width), BF16),
             short,
             pltpu.VMEM((2, chan_count, span, width), BF16),
-            pltpu.VMEM((2, rows, CHUNK, width), F32),
+            pltpu.VMEM((2, rows, CHUNK, width), BF16),
             pltpu.VMEM((chunks, 4, 8, span), F32),
             pltpu.VMEM((6, rows, width), F32),
             pltpu.VMEM((tm_count, 8, width), F32),
@@ -927,13 +975,13 @@
             pltpu.VMEM((2, tm_count, 8, LANE), F32),
             pltpu.VMEM((2, rows, width), F32),
             pltpu.VMEM((resets.shape[1], rows, LANE), jnp.int32),
-            dma((pieces,)), dma((pieces,)), dma((pieces,)), dma((pieces,)), dma((pieces,)), dma((pieces,)), dma((pieces,)),
-            dma((3,)), dma((2,)), dma((2,)), dma((2,)), dma((2,)),
-            dma((2,)), dma((2,)), dma((2, tm_count)), dma((2, tm_count)), dma((tm_count,)), dma(()),
+            dma(()), dma((pieces,)), dma(()), dma(()), dma(()), dma((pieces,)), dma(()),
+            dma((3,)), dma((2,)), dma((2,)), dma(()), dma((2,)),
+            dma((2,)), dma((2,)), dma((2,)), dma((2,)), dma(()), dma(()),
             pltpu.SemaphoreType.REGULAR,
             dma((2,)), dma((3, SENDS)), dma((SENDS,)), dma((3, SENDS)), dma((3, SENDS, 2)), dma((3, ring)), dma((SENDS,)),
             dma((SENDS,)), dma((ring,)), dma((ring, 7)), dma((2,)), dma((4, 2)), dma((2,)), dma((chunks,)),
-            dma((4, 3)), dma((4, 4)), dma((tm_count,)), dma((tm_count,)),
+            dma((4,)), dma((4,)), dma(()), dma(()),
         ],
         compiler_params=pltpu.CompilerParams(collective_id=0, has_side_effects=True, vmem_limit_bytes=VMEM_BYTES),
         name="whole",
@@ -942,53 +990,48 @@
 
 def tail_kernel(
     fin, in_grad, act, final, totals, wide_out, in_out, act_out, final_out, s0, s1, s2, s3, s4, s5,
-    fin_buf, wide_buf, in_buf, act_buf, fin_sem, wide_sem, in_sem, act_sem,
+    fin_buf, wide_buf, in_buf, in_wide, act_buf, load_sem, store_sem,
 ):
-    parts = fin_sem.shape[0]
-    size = fin.shape[0] // parts
-
     def move(src, dst, sem, i, n):
         at = pl.ds(i * n, n)
         return pltpu.make_async_copy(src.at[at], dst.at[at], sem)
 
-    loads = [move(fin, fin_buf, fin_sem.at[i], i, size) for i in range(parts)]
-    stores = [move(wide_buf, wide_out, wide_sem.at[i], i, size) for i in range(parts)]
-    pairs = []
-    for src, buf, dst, sem in ((in_grad, in_buf, in_out, in_sem), (act, act_buf, act_out, act_sem)):
-        n = sem.shape[1]
-        some = src.shape[0] // n
-        pairs += [(move(src, buf, sem.at[0, i], i, some), move(buf, dst, sem.at[1, i], i, some)) for i in range(n)]
-    for i in range(max(parts, len(pairs))):
-        if i < parts:
-            loads[i].start()
-        if i < len(pairs):
-            pairs[i][0].start()
+    jobs = []
+
+    def job(src, buf, wide, dst, parts):
+        n = src.shape[0] // parts
+        for i in range(parts):
+            k = len(jobs)
+            jobs.append((move(src, buf, load_sem.at[k], i, n), buf, wide, i * n, n, move(wide, dst, store_sem.at[k], i, n)))
+
+    job(fin, fin_buf, wide_buf, wide_out, TAIL)
+    job(in_grad, in_buf, in_wide, in_out, 2)
+    job(act, act_buf, act_buf, act_out, 2)
+    order = [0, 4, 1, 6, 2, 5, 3, 7] if TAIL == 4 else list(range(len(jobs)))
+    for k in order:
+        jobs[k][0].start()
     final_out[...] = final[...]
     for i, ref in enumerate((s0, s1, s2, s3, s4, s5)):
         ref[...] = totals[i : i + 1, :]
-    for i in range(max(parts, len(pairs))):
-        if i < parts:
-            loads[i].wait()
-
-            def cast(j, carry, i=i):
-                at = pl.ds(pl.multiple_of(i * size + j * 64, 64), 64)
-                wide_buf[at] = fin_buf[at].astype(F32)
+    for k in order:
+        load, buf, wide, start, n, store = jobs[k]
+        load.wait()
+        if buf is not wide:
+            step = 64 if len(buf.shape) == 2 else 1
+
+            def cast(j, carry, buf=buf, wide=wide, start=start, step=step):
+                at = pl.ds(start + j * step, step)
+                wide[at] = buf[at].astype(F32)
                 return carry
 
-            lax.fori_loop(0, size // 64, cast, 0, unroll=2)
-            stores[i].start()
-        if i < len(pairs):
-            pairs[i][0].wait()
-            pairs[i][1].start()
-    for copy in stores:
-        copy.wait()
-    for _, onward in pairs:
-        onward.wait()
+            lax.fori_loop(0, n // step, cast, 0, unroll=2)
+        store.start()
+    for k in order:
+        jobs[k][-1].wait()
 
 
 def tail(fin, in_grad, act, final, totals):
     width = fin.shape[-1]
-    flat = fin.reshape(-1, width)
     hbm = pl.BlockSpec(memory_space=pl.ANY)
     vmem = pl.BlockSpec(memory_space=pltpu.VMEM)
     dma = pltpu.SemaphoreType.DMA
@@ -996,7 +1039,7 @@
     return pl.pallas_call(
         tail_kernel,
         out_shape=(
-            jax.ShapeDtypeStruct(flat.shape, F32),
+            jax.ShapeDtypeStruct(fin.shape, F32),
             jax.ShapeDtypeStruct(in_grad.shape, F32),
             jax.ShapeDtypeStruct(act.shape, BF16),
             jax.ShapeDtypeStruct(final.shape, F32),
@@ -1004,13 +1047,13 @@
         in_specs=[hbm] * 3 + [vmem] * 2,
         out_specs=(hbm,) * 3 + (vmem,) * 7,
         scratch_shapes=[
-            pltpu.VMEM(flat.shape, BF16), pltpu.VMEM(flat.shape, F32),
-            pltpu.VMEM(in_grad.shape, F32), pltpu.VMEM(act.shape, BF16),
-            dma((TAIL,)), dma((TAIL,)), dma((2, 4)), dma((2, 2)),
+            pltpu.VMEM(fin.shape, BF16), pltpu.VMEM(fin.shape, F32),
+            pltpu.VMEM(in_grad.shape, BF16), pltpu.VMEM(in_grad.shape, F32), pltpu.VMEM(act.shape, BF16),
+            dma((TAIL + 4,)), dma((TAIL + 4,)),
         ],
         compiler_params=pltpu.CompilerParams(vmem_limit_bytes=VMEM_BYTES),
         name="tail",
-    )(flat, in_grad, act, final, totals)
+    )(fin, in_grad, act, final, totals)
 
 
 def body(

time: 206 us -> 203 us (0.985)
  Pallas kernels: 205 us -> 201 us
    pallas_call x1, Pallas kernels: 193 us -> 191 us  [layer(): pl.pallas_call(layer_kernel, out_shape=(jax.ShapeDtypeStruct((units * UNI...]
where the time goes in v5:
time: 203 us; the launch traced here: 202 us
  Pallas kernels  201 us (99%)
    pallas_call x1, Pallas kernels, layer(): pl.pallas_call(layer_kernel, out_shape=(jax.ShapeDtypeStruct((units * UNI...  191 us
    pallas_call x1, Pallas kernels, tail(): pl.pallas_call(tail_kernel, out_shape=(jax.ShapeDtypeStruct(fin.shape, F3...  10.7 us

profile of v5, /device:TPU:0, one launch (start us, length us, event | category | flops | bytes accessed | tf_op | source)
XLA Modules:
  0.0 202.1 jit_solution(1797704465726944486)
XLA Ops:
  0.6 190.8 %whole.1 = (bf16[6144,512]{1,0:T(8,128)(2,1)}, bf16[8,256,512]{2,1,0:T(8,128)(2,1)}, bf16[8,256,512]{2,1,0:T(8,128)(2,1)}, bf16[2048,2048]{1,0:T(8,128)(2,1)}, f32[8,512]{1,0:T(8,128)}, /*index=5*/f32[8,512]{1,0:T(8,128)}) custom-call(bf16[8,256,512]{2,1,0:T(8,128)(2,1)} %tokens.1, bf16[3,2048,512]{2,1,0:T(8,128)(2,1)} %weights.1, ...), custom_call_target="tpu_custom_call" | custom-call | tf_op jit(solution)/shard_map/whole/pallas_call | solution.py:941
  191.4 10.7 %tail.1 = (f32[6144,512]{1,0:T(8,128)}, f32[8,256,512]{2,1,0:T(8,128)}, bf16[8,256,512]{2,1,0:T(8,128)(2,1)}, f32[8,512]{1,0:T(8,128)}, f32[1,512]{1,0:T(1,128)}...) custom-call(bf16[6144,512]{1,0:T(8,128)(2,1)} %get-tuple-element.25.fin, ...), custom_call_target="tpu_custom_call" | custom-call | tf_op jit(solution)/shard_map/tail/pallas_call | solution.py:1039

commit v6 on v5

--- a/solution.py
+++ b/solution.py
@@ -9,6 +9,7 @@
 CHUNK = 32
 BLOCK = 16
 LANE = 128
+AHEAD = 4
 UNIT = 256
 LAG = 2
 PAIR = 80
@@ -155,7 +156,7 @@
     for copy in w_copies:
         copy.start()
     pl.semaphore_wait(barrier, tm_count + 2)
-    for ch in range(2):
+    for ch in range(AHEAD):
         for copy in token_copies(ch, 0, blocks, x_move):
             copy.start()
     lax.fori_loop(0, chunks, start_sibling, 0)
@@ -227,8 +228,8 @@
     def gather_step(ch, runs, h0=0, h1=blocks):
         entire = h1 - h0 == blocks
         if entire:
-            pl.when(ch + 2 < chunks - 1)(lambda: send_across(ch + 2))
-            pl.when(ch + 2 == chunks - 1)(send_last)
+            pl.when(ch + AHEAD < chunks - 1)(lambda: send_across(ch + AHEAD))
+            pl.when(ch + AHEAD == chunks - 1)(send_last)
             cot_copy(ch + 1).start()
 
         base = pl.multiple_of(ch * span, span)
@@ -435,7 +436,7 @@
             th = jnp.tanh(f * masked[at, cols] + (1.0 - f) * cand[at, cols])
             o = gate[at, cols]
             direct = cot[at, cols].astype(F32) * o * (1.0 - th * th)
-            side[at, cols] = o.astype(BF16)
+            side[at, cols] = jnp.where(o > 0.5, jnp.minimum(o - 1.0, -1e-30), o).astype(BF16)
             gate[at, cols] = direct
             keep = f * mask
             run, total = flow[0, :, cols], flow[1, :, cols]
@@ -460,8 +461,9 @@
             cols = lanes(j)
             f = forget[at, cols]
             th = jnp.tanh(f * masked[at, cols] + (1.0 - f) * cand[at, cols])
-            o = side[at, cols].astype(F32)
-            rest = 1.0 - o
+            q = side[at, cols].astype(F32)
+            o = jnp.where(q < 0.0, 1.0 + q, q)
+            rest = jnp.where(q < 0.0, -q, 1.0 - q)
             out = swapped(o * th + rest * own_tok[at, cols].astype(F32), BLOCK, rows).astype(BF16)
             act_buf[slot, :, pl.ds(t0, BLOCK), cols] = out.reshape(rows, BLOCK, LANE)
             side[at, cols] = (cot[at, cols].astype(F32) * rest).astype(BF16)
@@ -489,8 +491,8 @@
     n = tm_count // 2
     o, y = tm // 2, lax.rem(tm, 2)
     partner = (o * 2 + 1 - y, chan)
-    left = ((o - 1) * 2 + y, chan)
-    right = ((o + 1) * 2 + y, chan)
+    left = (lax.rem(o - 1 + n, n) * 2 + y, chan)
+    right = (lax.rem(o + 1, n) * 2 + y, chan)
     ring = ring_of(tm_count)
     ends, middle = (0, n - 1), (n // 2 - 1, n // 2)
     lines = [(0, middle[0] + y, n // 2, 1, None)]

time: 203 us -> 203 us (level)
  no operation moved by 1% of the time
where the time goes in v6:
time: 203 us; the launch traced here: 202 us
  Pallas kernels  202 us (100%)
    pallas_call x1, Pallas kernels, layer(): pl.pallas_call(layer_kernel, out_shape=(jax.ShapeDtypeStruct((units * UNI...  191 us
    pallas_call x1, Pallas kernels, tail(): pl.pallas_call(tail_kernel, out_shape=(jax.ShapeDtypeStruct(fin.shape, F3...  10.7 us

profile of v6, /device:TPU:0, one launch (start us, length us, event | category | flops | bytes accessed | tf_op | source)
XLA Modules:
  0.0 202.2 jit_solution(5110926568119455523)
XLA Ops:
  0.6 190.8 %whole.1 = (bf16[6144,512]{1,0:T(8,128)(2,1)}, bf16[8,256,512]{2,1,0:T(8,128)(2,1)}, bf16[8,256,512]{2,1,0:T(8,128)(2,1)}, bf16[2048,2048]{1,0:T(8,128)(2,1)}, f32[8,512]{1,0:T(8,128)}, /*index=5*/f32[8,512]{1,0:T(8,128)}) custom-call(bf16[8,256,512]{2,1,0:T(8,128)(2,1)} %tokens.1, bf16[3,2048,512]{2,1,0:T(8,128)(2,1)} %weights.1, ...), custom_call_target="tpu_custom_call" | custom-call | tf_op jit(solution)/shard_map/whole/pallas_call | solution.py:943
  191.5 10.7 %tail.1 = (f32[6144,512]{1,0:T(8,128)}, f32[8,256,512]{2,1,0:T(8,128)}, bf16[8,256,512]{2,1,0:T(8,128)(2,1)}, f32[8,512]{1,0:T(8,128)}, f32[1,512]{1,0:T(1,128)}...) custom-call(bf16[6144,512]{1,0:T(8,128)(2,1)} %get-tuple-element.25.fin, ...), custom_call_target="tpu_custom_call" | custom-call | tf_op jit(solution)/shard_map/tail/pallas_call | solution.py:1041

commit v7 on v6

--- a/solution.py
+++ b/solution.py
@@ -18,6 +18,7 @@
 VMEM_BYTES = 63 << 20
 TAIL = 4
 LATER = 4
+ADJOINT = 6
 OUTPUT = 8
 FIRST = 12
 MESH = pl.DeviceIdType.MESH
@@ -876,11 +877,11 @@
             lax.fori_loop(at, jnp.minimum(at + share, count), later, 0)
 
         pl.when(s == LATER - 1)(end_later)
-        pl.when(s == LATER + 1)(start_backward)
-        share = -(-count // (OUTPUT - LATER - 1))
-        at2 = (s - LATER - 1) * share
-
-        @pl.when(both(s > LATER, s < OUTPUT))
+        pl.when(s == ADJOINT)(start_backward)
+        share = -(-count // (OUTPUT - ADJOINT))
+        at2 = (s - ADJOINT) * share
+
+        @pl.when(both(s >= ADJOINT, s < OUTPUT))
         def _():
             lax.fori_loop(at2, jnp.minimum(at2 + share, count), backward, 0)
 

time: 203 us -> 201 us (level)
  no operation moved by 1% of the time
where the time goes in v7:
time: 201 us
  Pallas kernels  200 us (100%)
    pallas_call x1, Pallas kernels, layer(): pl.pallas_call(layer_kernel, out_shape=(jax.ShapeDtypeStruct((units * UNI...  189 us
    pallas_call x1, Pallas kernels, tail(): pl.pallas_call(tail_kernel, out_shape=(jax.ShapeDtypeStruct(fin.shape, F3...  10.7 us

profile of v7, /device:TPU:0, one launch (start us, length us, event | category | flops | bytes accessed | tf_op | source)
XLA Modules:
  0.0 200.6 jit_solution(5544350251494731456)
XLA Ops:
  0.6 189.2 %whole.1 = (bf16[6144,512]{1,0:T(8,128)(2,1)}, bf16[8,256,512]{2,1,0:T(8,128)(2,1)}, bf16[8,256,512]{2,1,0:T(8,128)(2,1)}, bf16[2048,2048]{1,0:T(8,128)(2,1)}, f32[8,512]{1,0:T(8,128)}, /*index=5*/f32[8,512]{1,0:T(8,128)}) custom-call(bf16[8,256,512]{2,1,0:T(8,128)(2,1)} %tokens.1, bf16[3,2048,512]{2,1,0:T(8,128)(2,1)} %weights.1, ...), custom_call_target="tpu_custom_call" | custom-call | tf_op jit(solution)/shard_map/whole/pallas_call | solution.py:944
  189.9 10.7 %tail.1 = (f32[6144,512]{1,0:T(8,128)}, f32[8,256,512]{2,1,0:T(8,128)}, bf16[8,256,512]{2,1,0:T(8,128)(2,1)}, f32[8,512]{1,0:T(8,128)}, f32[1,512]{1,0:T(1,128)}...) custom-call(bf16[6144,512]{1,0:T(8,128)(2,1)} %get-tuple-element.25.fin, ...), custom_call_target="tpu_custom_call" | custom-call | tf_op jit(solution)/shard_map/tail/pallas_call | solution.py:1042

commit v8 on v7

--- a/solution.py
+++ b/solution.py
@@ -16,7 +16,7 @@
 LINE = 48
 SENDS = 2
 VMEM_BYTES = 63 << 20
-TAIL = 4
+TAIL = 2
 LATER = 4
 ADJOINT = 6
 OUTPUT = 8
@@ -553,8 +553,15 @@
 
         make(u).start()
 
+    def rx_sem(u, place, l):
+        if isinstance(place, int):
+            which = (0, 1, 1, 2, 2, 3, 4)[place]
+        else:
+            which = jnp.where(place == 6, 4, 2)
+        return rx_recv.at[lax.rem(u, ring), which]
+
     def to_rx(src, u, place, l, sem, target):
-        return remote(src, rx.at[rx_rows(u, place, l)], sem, rx_recv.at[lax.rem(u, ring), place], target)
+        return remote(src, rx.at[rx_rows(u, place, l)], sem, rx_sem(u, place, l), target)
 
     def pair_copy(u):
         return to_rx(raw.at[wg_rows(0, u, True)], u, 0, 0, pair_send.at[lax.rem(u, SENDS)], partner)
@@ -571,6 +578,13 @@
         at = rx_rows(u, place, l)
         to_rx(rx.at[at], u, place, l, red_send.at[l, 0], partner).wait_recv()
         return rx[at].astype(F32)
+
+    def red_wait_both(l, u):
+        place, size = (1, PAIR) if l == 0 else (3, LINE)
+        start = rx_rows(u, place, l).start
+        at = rx.at[pl.ds(start, 2 * size)]
+        remote(at, at, red_send.at[l, 0], rx_sem(u, place, l), partner).wait_recv()
+        return [rx[pl.ds(pl.multiple_of(start + i * size, 16), size)].astype(F32) for i in range(2)]
 
     def bc_copy(l, u, to_right, src):
         return remote(
@@ -820,9 +834,9 @@
             @pl.when(both(o == c, go))
             def _(l=l, c=c, u=u):
                 if l == 0 and n > 2:
-                    add_to(l, u, red_wait(l, c, u, 0), red_wait(l, c, u, 1))
+                    add_to(l, u, *red_wait_both(l, u))
                 elif l > 0 and 0 < c < n - 1:
-                    add_to(l, u, red_wait(l, c, u, 0), red_wait(l, c, u, 1))
+                    add_to(l, u, *red_wait_both(l, u))
                 else:
                     pl.when(o > 0)(lambda: add_to(l, u, red_wait(l, c, u, 0)))
                     pl.when(o < n - 1)(lambda: add_to(l, u, red_wait(l, c, u, 1)))
@@ -983,7 +997,7 @@
             dma((2,)), dma((2,)), dma((2,)), dma((2,)), dma(()), dma(()),
             pltpu.SemaphoreType.REGULAR,
             dma((2,)), dma((3, SENDS)), dma((SENDS,)), dma((3, SENDS)), dma((3, SENDS, 2)), dma((3, ring)), dma((SENDS,)),
-            dma((SENDS,)), dma((ring,)), dma((ring, 7)), dma((2,)), dma((4, 2)), dma((2,)), dma((chunks,)),
+            dma((SENDS,)), dma((ring,)), dma((ring, 5)), dma((2,)), dma((4, 2)), dma((2,)), dma((chunks,)),
             dma((4,)), dma((4,)), dma(()), dma(()),
         ],
         compiler_params=pltpu.CompilerParams(collective_id=0, has_side_effects=True, vmem_limit_bytes=VMEM_BYTES),

time: 201 us -> 201 us (level)
  no operation moved by 1% of the time
where the time goes in v8:
time: 201 us; the launch traced here: 200 us
  Pallas kernels  199 us (99%)
    pallas_call x1, Pallas kernels, layer(): pl.pallas_call(layer_kernel, out_shape=(jax.ShapeDtypeStruct((units * UNI...  189 us
    pallas_call x1, Pallas kernels, tail(): pl.pallas_call(tail_kernel, out_shape=(jax.ShapeDtypeStruct(fin.shape, F3...  10.5 us

profile of v8, /device:TPU:0, one launch (start us, length us, event | category | flops | bytes accessed | tf_op | source)
XLA Modules:
  0.0 200.1 jit_solution(7606273651504289498)
XLA Ops:
  0.6 189.0 %whole.1 = (bf16[6144,512]{1,0:T(8,128)(2,1)}, bf16[8,256,512]{2,1,0:T(8,128)(2,1)}, bf16[8,256,512]{2,1,0:T(8,128)(2,1)}, bf16[2048,2048]{1,0:T(8,128)(2,1)}, f32[8,512]{1,0:T(8,128)}, /*index=5*/f32[8,512]{1,0:T(8,128)}) custom-call(bf16[8,256,512]{2,1,0:T(8,128)(2,1)} %tokens.1, bf16[3,2048,512]{2,1,0:T(8,128)(2,1)} %weights.1, ...), custom_call_target="tpu_custom_call" | custom-call | tf_op jit(solution)/shard_map/whole/pallas_call | solution.py:958
  189.6 10.5 %tail.1 = (f32[6144,512]{1,0:T(8,128)}, f32[8,256,512]{2,1,0:T(8,128)}, bf16[8,256,512]{2,1,0:T(8,128)(2,1)}, f32[8,512]{1,0:T(8,128)}, f32[1,512]{1,0:T(1,128)}...) custom-call(bf16[6144,512]{1,0:T(8,128)(2,1)} %get-tuple-element.25.fin, ...), custom_call_target="tpu_custom_call" | custom-call | tf_op jit(solution)/shard_map/tail/pallas_call | solution.py:1056
